TPU v7x, 32 devices: a whole 2x2x4 slice. The times are simulated.
32 devices in a mesh: dp: 2 (over x), ctx: 16 (over z, y, core).
Axes of the slice: x: 2, y: 2, z: 4, core: 2. Of those that a mesh axis runs over, the one named last changes fastest.
Arguments:
- query_act: bfloat16 [2, 2048, 2048], P('dp', 'ctx'), may hold values from -6 to 6
- key_act: bfloat16 [2, 2048, 2048], P('dp', 'ctx'), may hold values from -6 to 6
- value_act: bfloat16 [2, 2048, 2048], P('dp', 'ctx'), may hold values from -6 to 6
- grad_out: bfloat16 [2, 2048, 2048], P('dp', 'ctx'), may hold values from -6 to 6
- filter_taps: bfloat16 [128, 2048], replicated, may hold values from -2.5 to 2.5
Outputs:
- output_act: bfloat16 [2, 2048, 2048], P('dp', 'ctx')
- grad_query: bfloat16 [2, 2048, 2048], P('dp', 'ctx')
- grad_key: bfloat16 [2, 2048, 2048], P('dp', 'ctx')
- grad_value: bfloat16 [2, 2048, 2048], P('dp', 'ctx')
- grad_filter: float32 [128, 2048], P(None, 'ctx')
All inputs are finite; a program needn't handle non-finite values.
Results may differ from a plain program's by a relative error of at most 0.0065.
Values may be sent and summed in bfloat16 or wider, within the bound.
No kernel may reach another device: no remote copies, remote signals or barrier semaphores. Data moves between devices by JAX's collectives and lax.ppermute only.
A program may use at most 64 MiB of HBM per device.

v0:
```python
import math

import jax
import jax.numpy as jnp
from jax import lax
from jax.sharding import PartitionSpec as P

tap_block = 16


def from_behind(array, axis, by):
    devices = lax.axis_size(axis)
    pairs = [(i, i + by) for i in range(devices) if 0 <= i + by < devices]
    return lax.ppermute(array, axis, pairs)


def forward_taps(padded, weights, length):
    tap_count = weights.shape[0]

    def forward_advance(number, running):
        first = number * tap_block
        window = lax.dynamic_slice_in_dim(
            padded, tap_count - tap_block - first, length + tap_block - 1, 0
        )
        coeffs = lax.dynamic_slice_in_dim(weights, first, tap_block, 0)
        for inner in range(tap_block):
            start_row = tap_block - 1 - inner
            running = running + coeffs[inner] * window[start_row : start_row + length]
        return running

    initial = jnp.zeros((length, padded.shape[1]), jnp.float32)
    return lax.fori_loop(0, tap_count // tap_block, forward_advance, initial)


def backward_taps(extended, weights, length):
    tap_count = weights.shape[0]

    def backward_advance(number, running):
        first = number * tap_block
        window = lax.dynamic_slice_in_dim(extended, first, length + tap_block - 1, 0)
        coeffs = lax.dynamic_slice_in_dim(weights, first, tap_block, 0)
        for inner in range(tap_block):
            running = running + coeffs[inner] * window[inner : inner + length]
        return running

    initial = jnp.zeros((length, extended.shape[1]), jnp.float32)
    return lax.fori_loop(0, tap_count // tap_block, backward_advance, initial)


def lag_sums(grad_float, padded, tap_count):
    length = grad_float.shape[0]

    def lag_advance(number, running):
        first = number * tap_block
        window = lax.dynamic_slice_in_dim(
            padded, tap_count - tap_block - first, length + tap_block - 1, 0
        )
        lines = []
        for inner in range(tap_block):
            start_row = tap_block - 1 - inner
            lines.append(jnp.sum(grad_float * window[start_row : start_row + length], axis=0))
        return lax.dynamic_update_slice_in_dim(running, jnp.stack(lines), first, 0)

    initial = jnp.zeros((tap_count, padded.shape[1]), jnp.float32)
    return lax.fori_loop(0, tap_count // tap_block, lag_advance, initial)


def per_device(query_act, key_act, value_act, grad_out, filter_taps):
    query_rows = query_act[0].astype(jnp.float32)
    key_rows = key_act[0].astype(jnp.float32)
    value_rows = value_act[0].astype(jnp.float32)
    grad_rows = grad_out[0].astype(jnp.float32)
    length = query_rows.shape[0]
    channels = query_rows.shape[1]
    tap_count = filter_taps.shape[0]
    weights = filter_taps.astype(jnp.float32)
    kv_product = (key_rows * value_rows).astype(jnp.bfloat16)
    gate_grad = (grad_rows * query_rows).astype(jnp.bfloat16)
    before = from_behind(kv_product[length - tap_count + 1 :], "ctx", 1)
    beyond = from_behind(gate_grad[: tap_count - 1], "ctx", -1)
    padded = jnp.concatenate([before, kv_product], axis=0)
    filtered = forward_taps(padded, weights, length)
    output_rows = (query_rows * filtered).astype(jnp.bfloat16)
    grad_query_rows = (grad_rows * filtered).astype(jnp.bfloat16)
    extended = jnp.concatenate([gate_grad, beyond], axis=0)
    flowing = backward_taps(extended, weights, length)
    grad_key_rows = (flowing * value_rows).astype(jnp.bfloat16)
    grad_value_rows = (flowing * key_rows).astype(jnp.bfloat16)
    token_count = length * lax.axis_size("ctx") * lax.axis_size("dp")
    partial_sum = lag_sums(gate_grad.astype(jnp.float32), padded, tap_count) * (
        1.0 / math.sqrt(token_count)
    )
    share_width = channels // lax.axis_size("ctx")
    summed = lax.psum(partial_sum, ("dp", "ctx"))
    own_filter = lax.dynamic_slice_in_dim(
        summed, lax.axis_index("ctx") * share_width, share_width, 1
    )
    return (
        output_rows[None],
        grad_query_rows[None],
        grad_key_rows[None],
        grad_value_rows[None],
        own_filter,
    )


def solution(mesh):
    in_specs = (
        P("dp", "ctx", None),
        P("dp", "ctx", None),
        P("dp", "ctx", None),
        P("dp", "ctx", None),
        P(),
    )
    out_specs = (
        P("dp", "ctx", None),
        P("dp", "ctx", None),
        P("dp", "ctx", None),
        P("dp", "ctx", None),
        P(None, "ctx"),
    )
    return jax.shard_map(
        per_device, mesh=mesh, in_specs=in_specs, out_specs=out_specs, check_vma=False
    )
```

profile of v0, /device:TPU:0, one launch (start us, length us, event | category | flops | bytes accessed | tf_op | source)
XLA Modules:
  0.0 262.6 jit_solution(804350308680590192)
XLA Ops:
  7.2 1.4 fusion.40
  8.6 1.3 collective-permute-start.1
  10.0 1.1 convert_element_type.482
  11.1 1.5 collective-permute-done.1
  12.6 1.3 pad_maximum_fusion.1
  13.9 42.1 %while.47 = (s32[]{:T(128)}, f32[128,2048]{1,0:T(8,128)S(1)}, f32[128,2048]{1,0:T(8,128)}, bf16[255,2048]{1,0:T(8,128)(2,1)S(1)}, s32[]{:T(128)}, /*index=5*/s32...) while((s32[]{:T(128)}, f32[128,2048]{1,0:T(8,128)S(1)}, ...), condition=%wide.region_3.0_spmd.clone, body=%wide.region_2.0_spmd.clone.sunk | while | flops 12845095 | bytes 10879758 | solution.py:47
  13.9 1.7 constant_dynamic-slice_fusion.36
  15.6 3.4 %fusion.45 = f32[128,2048]{1,0:T(8,128)S(1)} fusion(f32[128,2048]{1,0:T(8,128)S(1)} %get-tuple-element.612, bf16[255,2048]{1,0:T(8,128)(2,1)S(1)} %get-tuple-element.638, s32[]{:T(128)S(6)} %add.1214, s32[]{:T(128)S(6)} %add.1215, s32[]{:T(128)S(6)} %add.1216, s32[]{:T(128)S(6)} %add.1217, s32[]{:T(128)S(6)} %add.1218, s32[]{:T(128)S(6)} %add.1219, ...), kind=kLoop, calls=%fused_computation.64.clone.1 | loop fusion | flops 12845056 | bytes 10616897 | tf_op jit(solution)/shard_map/while/body/eval_jaxpr/add | solution.py:43
  19.0 1.9 constant_dynamic-slice_fusion.36
  21.0 3.4 %fusion.45 = f32[128,2048]{1,0:T(8,128)S(1)} fusion(f32[128,2048]{1,0:T(8,128)S(1)} %get-tuple-element.612, bf16[255,2048]{1,0:T(8,128)(2,1)S(1)} %get-tuple-element.638, s32[]{:T(128)S(6)} %add.1214, s32[]{:T(128)S(6)} %add.1215, s32[]{:T(128)S(6)} %add.1216, s32[]{:T(128)S(6)} %add.1217, s32[]{:T(128)S(6)} %add.1218, s32[]{:T(128)S(6)} %add.1219, ...), kind=kLoop, calls=%fused_computation.64.clone.1 | loop fusion | flops 12845056 | bytes 10616897 | tf_op jit(solution)/shard_map/while/body/eval_jaxpr/add | solution.py:43
  24.4 1.7 constant_dynamic-slice_fusion.36
  26.1 3.4 %fusion.45 = f32[128,2048]{1,0:T(8,128)S(1)} fusion(f32[128,2048]{1,0:T(8,128)S(1)} %get-tuple-element.612, bf16[255,2048]{1,0:T(8,128)(2,1)S(1)} %get-tuple-element.638, s32[]{:T(128)S(6)} %add.1214, s32[]{:T(128)S(6)} %add.1215, s32[]{:T(128)S(6)} %add.1216, s32[]{:T(128)S(6)} %add.1217, s32[]{:T(128)S(6)} %add.1218, s32[]{:T(128)S(6)} %add.1219, ...), kind=kLoop, calls=%fused_computation.64.clone.1 | loop fusion | flops 12845056 | bytes 10616897 | tf_op jit(solution)/shard_map/while/body/eval_jaxpr/add | solution.py:43
  29.5 1.9 constant_dynamic-slice_fusion.36
  31.5 3.4 %fusion.45 = f32[128,2048]{1,0:T(8,128)S(1)} fusion(f32[128,2048]{1,0:T(8,128)S(1)} %get-tuple-element.612, bf16[255,2048]{1,0:T(8,128)(2,1)S(1)} %get-tuple-element.638, s32[]{:T(128)S(6)} %add.1214, s32[]{:T(128)S(6)} %add.1215, s32[]{:T(128)S(6)} %add.1216, s32[]{:T(128)S(6)} %add.1217, s32[]{:T(128)S(6)} %add.1218, s32[]{:T(128)S(6)} %add.1219, ...), kind=kLoop, calls=%fused_computation.64.clone.1 | loop fusion | flops 12845056 | bytes 10616897 | tf_op jit(solution)/shard_map/while/body/eval_jaxpr/add | solution.py:43
  34.9 1.7 constant_dynamic-slice_fusion.36
  36.6 3.4 %fusion.45 = f32[128,2048]{1,0:T(8,128)S(1)} fusion(f32[128,2048]{1,0:T(8,128)S(1)} %get-tuple-element.612, bf16[255,2048]{1,0:T(8,128)(2,1)S(1)} %get-tuple-element.638, s32[]{:T(128)S(6)} %add.1214, s32[]{:T(128)S(6)} %add.1215, s32[]{:T(128)S(6)} %add.1216, s32[]{:T(128)S(6)} %add.1217, s32[]{:T(128)S(6)} %add.1218, s32[]{:T(128)S(6)} %add.1219, ...), kind=kLoop, calls=%fused_computation.64.clone.1 | loop fusion | flops 12845056 | bytes 10616897 | tf_op jit(solution)/shard_map/while/body/eval_jaxpr/add | solution.py:43
  40.1 1.9 constant_dynamic-slice_fusion.36
  42.0 3.4 %fusion.45 = f32[128,2048]{1,0:T(8,128)S(1)} fusion(f32[128,2048]{1,0:T(8,128)S(1)} %get-tuple-element.612, bf16[255,2048]{1,0:T(8,128)(2,1)S(1)} %get-tuple-element.638, s32[]{:T(128)S(6)} %add.1214, s32[]{:T(128)S(6)} %add.1215, s32[]{:T(128)S(6)} %add.1216, s32[]{:T(128)S(6)} %add.1217, s32[]{:T(128)S(6)} %add.1218, s32[]{:T(128)S(6)} %add.1219, ...), kind=kLoop, calls=%fused_computation.64.clone.1 | loop fusion | flops 12845056 | bytes 10616897 | tf_op jit(solution)/shard_map/while/body/eval_jaxpr/add | solution.py:43
  45.5 1.7 constant_dynamic-slice_fusion.36
  47.2 3.4 %fusion.45 = f32[128,2048]{1,0:T(8,128)S(1)} fusion(f32[128,2048]{1,0:T(8,128)S(1)} %get-tuple-element.612, bf16[255,2048]{1,0:T(8,128)(2,1)S(1)} %get-tuple-element.638, s32[]{:T(128)S(6)} %add.1214, s32[]{:T(128)S(6)} %add.1215, s32[]{:T(128)S(6)} %add.1216, s32[]{:T(128)S(6)} %add.1217, s32[]{:T(128)S(6)} %add.1218, s32[]{:T(128)S(6)} %add.1219, ...), kind=kLoop, calls=%fused_computation.64.clone.1 | loop fusion | flops 12845056 | bytes 10616897 | tf_op jit(solution)/shard_map/while/body/eval_jaxpr/add | solution.py:43
  50.6 2.0 constant_dynamic-slice_fusion.36
  52.6 3.4 %fusion.45 = f32[128,2048]{1,0:T(8,128)S(1)} fusion(f32[128,2048]{1,0:T(8,128)S(1)} %get-tuple-element.612, bf16[255,2048]{1,0:T(8,128)(2,1)S(1)} %get-tuple-element.638, s32[]{:T(128)S(6)} %add.1214, s32[]{:T(128)S(6)} %add.1215, s32[]{:T(128)S(6)} %add.1216, s32[]{:T(128)S(6)} %add.1217, s32[]{:T(128)S(6)} %add.1218, s32[]{:T(128)S(6)} %add.1219, ...), kind=kLoop, calls=%fused_computation.64.clone.1 | loop fusion | flops 12845056 | bytes 10616897 | tf_op jit(solution)/shard_map/while/body/eval_jaxpr/add | solution.py:43
  56.0 2.5 fusion.36
  58.6 10.7 %collective-permute-start = (bf16[127,2048]{1,0:T(8,128)(2,1)S(1)}, bf16[127,2048]{1,0:T(8,128)(2,1)}, u32[]{:S(2)}, u32[]{:S(2)}) collective-permute-start(bf16[127,2048]{1,0:T(8,128)(2,1)S(1)} %slice.776), channel_id=1, source_target_pairs={{0,1},{1,2},{2,3},{3,4},{4,5},{5,6},{6,7},{7,8},{8,9},{9,10},{10,1... | collective-permute-start | bytes 1560584 | tf_op jit(solution)/shard_map/ppermute | solution.py:14
  69.4 0.8 collective-permute-done
  70.2 1.4 pad_maximum_fusion
  71.6 1.1 broadcast.3
  72.7 41.9 %while.45 = (s32[]{:T(128)}, f32[128,2048]{1,0:T(8,128)}, bf16[255,2048]{1,0:T(8,128)(2,1)S(1)}, f32[128,2048]{1,0:T(8,128)S(1)}, s32[]{:T(128)}, /*index=5*/s32...) while((s32[]{:T(128)}, f32[128,2048]{1,0:T(8,128)}, ...), condition=%wide.region_21.0_spmd, body=%wide.region_4.0_spmd.sunk | while | flops 12550169 | bytes 10093105 | solution.py:65
  72.7 4.3 %multiply_reduce_fusion.17 = (f32[2048]{0:T(1024)S(1)}, f32[2048]{0:T(1024)S(1)}, f32[2048]{0:T(1024)S(1)}, f32[2048]{0:T(1024)S(1)}, f32[2048]{0:T(1024)S(1)}, ...) fusion(f32[128,2048]{1,0:T(8,128)S(1)} %get-tuple-element.787, ...), kind=kLoop, calls=%fused_computation.clone.1 | loop fusion | flops 12550144 | bytes 9568320 | tf_op jit(solution)/shard_map/while/body/eval_jaxpr/reduce_sum | solution.py:61
  77.3 0.7 constant_dynamic-update-slice_fusion.2
  77.9 4.3 %multiply_reduce_fusion.17 = (f32[2048]{0:T(1024)S(1)}, f32[2048]{0:T(1024)S(1)}, f32[2048]{0:T(1024)S(1)}, f32[2048]{0:T(1024)S(1)}, f32[2048]{0:T(1024)S(1)}, ...) fusion(f32[128,2048]{1,0:T(8,128)S(1)} %get-tuple-element.787, ...), kind=kLoop, calls=%fused_computation.clone.1 | loop fusion | flops 12550144 | bytes 9568320 | tf_op jit(solution)/shard_map/while/body/eval_jaxpr/reduce_sum | solution.py:61
  82.5 0.7 constant_dynamic-update-slice_fusion.2
  83.1 4.3 %multiply_reduce_fusion.17 = (f32[2048]{0:T(1024)S(1)}, f32[2048]{0:T(1024)S(1)}, f32[2048]{0:T(1024)S(1)}, f32[2048]{0:T(1024)S(1)}, f32[2048]{0:T(1024)S(1)}, ...) fusion(f32[128,2048]{1,0:T(8,128)S(1)} %get-tuple-element.787, ...), kind=kLoop, calls=%fused_computation.clone.1 | loop fusion | flops 12550144 | bytes 9568320 | tf_op jit(solution)/shard_map/while/body/eval_jaxpr/reduce_sum | solution.py:61
  87.7 0.7 constant_dynamic-update-slice_fusion.2
  88.4 4.3 %multiply_reduce_fusion.17 = (f32[2048]{0:T(1024)S(1)}, f32[2048]{0:T(1024)S(1)}, f32[2048]{0:T(1024)S(1)}, f32[2048]{0:T(1024)S(1)}, f32[2048]{0:T(1024)S(1)}, ...) fusion(f32[128,2048]{1,0:T(8,128)S(1)} %get-tuple-element.787, ...), kind=kLoop, calls=%fused_computation.clone.1 | loop fusion | flops 12550144 | bytes 9568320 | tf_op jit(solution)/shard_map/while/body/eval_jaxpr/reduce_sum | solution.py:61
  92.9 0.7 constant_dynamic-update-slice_fusion.2
  93.6 4.3 %multiply_reduce_fusion.17 = (f32[2048]{0:T(1024)S(1)}, f32[2048]{0:T(1024)S(1)}, f32[2048]{0:T(1024)S(1)}, f32[2048]{0:T(1024)S(1)}, f32[2048]{0:T(1024)S(1)}, ...) fusion(f32[128,2048]{1,0:T(8,128)S(1)} %get-tuple-element.787, ...), kind=kLoop, calls=%fused_computation.clone.1 | loop fusion | flops 12550144 | bytes 9568320 | tf_op jit(solution)/shard_map/while/body/eval_jaxpr/reduce_sum | solution.py:61
  98.8 4.3 %multiply_reduce_fusion.17 = (f32[2048]{0:T(1024)S(1)}, f32[2048]{0:T(1024)S(1)}, f32[2048]{0:T(1024)S(1)}, f32[2048]{0:T(1024)S(1)}, f32[2048]{0:T(1024)S(1)}, ...) fusion(f32[128,2048]{1,0:T(8,128)S(1)} %get-tuple-element.787, ...), kind=kLoop, calls=%fused_computation.clone.1 | loop fusion | flops 12550144 | bytes 9568320 | tf_op jit(solution)/shard_map/while/body/eval_jaxpr/reduce_sum | solution.py:61
  103.4 0.7 constant_dynamic-update-slice_fusion.2
  104.1 4.3 %multiply_reduce_fusion.17 = (f32[2048]{0:T(1024)S(1)}, f32[2048]{0:T(1024)S(1)}, f32[2048]{0:T(1024)S(1)}, f32[2048]{0:T(1024)S(1)}, f32[2048]{0:T(1024)S(1)}, ...) fusion(f32[128,2048]{1,0:T(8,128)S(1)} %get-tuple-element.787, ...), kind=kLoop, calls=%fused_computation.clone.1 | loop fusion | flops 12550144 | bytes 9568320 | tf_op jit(solution)/shard_map/while/body/eval_jaxpr/reduce_sum | solution.py:61
  108.6 0.7 constant_dynamic-update-slice_fusion.2
  109.3 4.3 %multiply_reduce_fusion.17 = (f32[2048]{0:T(1024)S(1)}, f32[2048]{0:T(1024)S(1)}, f32[2048]{0:T(1024)S(1)}, f32[2048]{0:T(1024)S(1)}, f32[2048]{0:T(1024)S(1)}, ...) fusion(f32[128,2048]{1,0:T(8,128)S(1)} %get-tuple-element.787, ...), kind=kLoop, calls=%fused_computation.clone.1 | loop fusion | flops 12550144 | bytes 9568320 | tf_op jit(solution)/shard_map/while/body/eval_jaxpr/reduce_sum | solution.py:61
  113.9 0.7 constant_dynamic-update-slice_fusion.2
  114.5 2.4 broadcast_multiply_fusion
  116.9 42.6 %while.46 = (s32[]{:T(128)}, f32[128,2048]{1,0:T(8,128)S(1)}, f32[128,2048]{1,0:T(8,128)}, bf16[255,2048]{1,0:T(8,128)(2,1)S(1)}, s32[]{:T(128)}, /*index=5*/s32...) while((s32[]{:T(128)}, f32[128,2048]{1,0:T(8,128)S(1)}, ...), condition=%wide.region_1.0_spmd.clone, body=%wide.region_0.0_spmd.clone.sunk | while | flops 12845097 | bytes 10879787 | solution.py:32
  117.0 1.7 constant_dynamic-slice_fusion.35
  118.7 3.5 %fusion.44 = f32[128,2048]{1,0:T(8,128)S(1)} fusion(f32[128,2048]{1,0:T(8,128)S(1)} %get-tuple-element.685, bf16[255,2048]{1,0:T(8,128)(2,1)S(1)} %get-tuple-element.712, s32[]{:T(128)S(6)} %select_n.70, s32[]{:T(128)S(6)} %add.1165, s32[]{:T(128)S(6)} %add.1166, s32[]{:T(128)S(6)} %add.1167, s32[]{:T(128)S(6)} %add.1168, s32[]{:T(128)S(6)} %add.1169, ...), kind=kLoop, calls=%fused_computation.32.clone.1 | loop fusion | flops 12845056 | bytes 10616897 | tf_op jit(solution)/shard_map/while/body/eval_jaxpr/add | solution.py:28
  122.1 1.9 constant_dynamic-slice_fusion.35
  124.1 3.5 %fusion.44 = f32[128,2048]{1,0:T(8,128)S(1)} fusion(f32[128,2048]{1,0:T(8,128)S(1)} %get-tuple-element.685, bf16[255,2048]{1,0:T(8,128)(2,1)S(1)} %get-tuple-element.712, s32[]{:T(128)S(6)} %select_n.70, s32[]{:T(128)S(6)} %add.1165, s32[]{:T(128)S(6)} %add.1166, s32[]{:T(128)S(6)} %add.1167, s32[]{:T(128)S(6)} %add.1168, s32[]{:T(128)S(6)} %add.1169, ...), kind=kLoop, calls=%fused_computation.32.clone.1 | loop fusion | flops 12845056 | bytes 10616897 | tf_op jit(solution)/shard_map/while/body/eval_jaxpr/add | solution.py:28
  127.6 1.7 constant_dynamic-slice_fusion.35
  129.3 3.5 %fusion.44 = f32[128,2048]{1,0:T(8,128)S(1)} fusion(f32[128,2048]{1,0:T(8,128)S(1)} %get-tuple-element.685, bf16[255,2048]{1,0:T(8,128)(2,1)S(1)} %get-tuple-element.712, s32[]{:T(128)S(6)} %select_n.70, s32[]{:T(128)S(6)} %add.1165, s32[]{:T(128)S(6)} %add.1166, s32[]{:T(128)S(6)} %add.1167, s32[]{:T(128)S(6)} %add.1168, s32[]{:T(128)S(6)} %add.1169, ...), kind=kLoop, calls=%fused_computation.32.clone.1 | loop fusion | flops 12845056 | bytes 10616897 | tf_op jit(solution)/shard_map/while/body/eval_jaxpr/add | solution.py:28
  132.7 1.9 constant_dynamic-slice_fusion.35
  134.7 3.5 %fusion.44 = f32[128,2048]{1,0:T(8,128)S(1)} fusion(f32[128,2048]{1,0:T(8,128)S(1)} %get-tuple-element.685, bf16[255,2048]{1,0:T(8,128)(2,1)S(1)} %get-tuple-element.712, s32[]{:T(128)S(6)} %select_n.70, s32[]{:T(128)S(6)} %add.1165, s32[]{:T(128)S(6)} %add.1166, s32[]{:T(128)S(6)} %add.1167, s32[]{:T(128)S(6)} %add.1168, s32[]{:T(128)S(6)} %add.1169, ...), kind=kLoop, calls=%fused_computation.32.clone.1 | loop fusion | flops 12845056 | bytes 10616897 | tf_op jit(solution)/shard_map/while/body/eval_jaxpr/add | solution.py:28
  138.2 1.7 constant_dynamic-slice_fusion.35
  139.9 3.5 %fusion.44 = f32[128,2048]{1,0:T(8,128)S(1)} fusion(f32[128,2048]{1,0:T(8,128)S(1)} %get-tuple-element.685, bf16[255,2048]{1,0:T(8,128)(2,1)S(1)} %get-tuple-element.712, s32[]{:T(128)S(6)} %select_n.70, s32[]{:T(128)S(6)} %add.1165, s32[]{:T(128)S(6)} %add.1166, s32[]{:T(128)S(6)} %add.1167, s32[]{:T(128)S(6)} %add.1168, s32[]{:T(128)S(6)} %add.1169, ...), kind=kLoop, calls=%fused_computation.32.clone.1 | loop fusion | flops 12845056 | bytes 10616897 | tf_op jit(solution)/shard_map/while/body/eval_jaxpr/add | solution.py:28
  143.4 1.9 constant_dynamic-slice_fusion.35
  145.4 3.5 %fusion.44 = f32[128,2048]{1,0:T(8,128)S(1)} fusion(f32[128,2048]{1,0:T(8,128)S(1)} %get-tuple-element.685, bf16[255,2048]{1,0:T(8,128)(2,1)S(1)} %get-tuple-element.712, s32[]{:T(128)S(6)} %select_n.70, s32[]{:T(128)S(6)} %add.1165, s32[]{:T(128)S(6)} %add.1166, s32[]{:T(128)S(6)} %add.1167, s32[]{:T(128)S(6)} %add.1168, s32[]{:T(128)S(6)} %add.1169, ...), kind=kLoop, calls=%fused_computation.32.clone.1 | loop fusion | flops 12845056 | bytes 10616897 | tf_op jit(solution)/shard_map/while/body/eval_jaxpr/add | solution.py:28
  148.9 1.7 constant_dynamic-slice_fusion.35
  150.6 3.5 %fusion.44 = f32[128,2048]{1,0:T(8,128)S(1)} fusion(f32[128,2048]{1,0:T(8,128)S(1)} %get-tuple-element.685, bf16[255,2048]{1,0:T(8,128)(2,1)S(1)} %get-tuple-element.712, s32[]{:T(128)S(6)} %select_n.70, s32[]{:T(128)S(6)} %add.1165, s32[]{:T(128)S(6)} %add.1166, s32[]{:T(128)S(6)} %add.1167, s32[]{:T(128)S(6)} %add.1168, s32[]{:T(128)S(6)} %add.1169, ...), kind=kLoop, calls=%fused_computation.32.clone.1 | loop fusion | flops 12845056 | bytes 10616897 | tf_op jit(solution)/shard_map/while/body/eval_jaxpr/add | solution.py:28
  154.1 2.0 constant_dynamic-slice_fusion.35
  156.1 3.5 %fusion.44 = f32[128,2048]{1,0:T(8,128)S(1)} fusion(f32[128,2048]{1,0:T(8,128)S(1)} %get-tuple-element.685, bf16[255,2048]{1,0:T(8,128)(2,1)S(1)} %get-tuple-element.712, s32[]{:T(128)S(6)} %select_n.70, s32[]{:T(128)S(6)} %add.1165, s32[]{:T(128)S(6)} %add.1166, s32[]{:T(128)S(6)} %add.1167, s32[]{:T(128)S(6)} %add.1168, s32[]{:T(128)S(6)} %add.1169, ...), kind=kLoop, calls=%fused_computation.32.clone.1 | loop fusion | flops 12845056 | bytes 10616897 | tf_op jit(solution)/shard_map/while/body/eval_jaxpr/add | solution.py:28
  159.5 1.2 fusion.39
  160.8 93.5 %all-reduce.2.cloned.1.call-done = f32[128,2048]{1,0:T(8,128)} async-done(((f32[128,2048]{1,0:T(8,128)}), f32[128,2048]{1,0:T(8,128)}) %all-reduce.2.cloned.1.call-update) | async-done | bytes 1048592 | tf_op jit(solution)/shard_map/psum | solution.py:94
  254.3 1.5 constant_dynamic-slice_fusion.32
  (24 shorter events, 2.6 us)
Async XLA Ops:
  7.2 2.8 %copy-start.4 = (bf16[128,2048]{1,0:T(8,128)(2,1)S(1)}, bf16[128,2048]{1,0:T(8,128)(2,1)}, u32[]{:S(2)}) copy-start(bf16[128,2048]{1,0:T(8,128)(2,1)} %param.15) | copy-start | bytes 1572868
  7.2 247.1 %all-reduce.2.cloned.1.call-start = ((), (), s32[]{:S(2)}) async-start(), calls=%async_computation | async-start | bytes 2097152 | tf_op jit(solution)/shard_map/psum | solution.py:94
  8.6 2.4 copy-start.3
  8.6 3.9 %collective-permute-start.1 = (bf16[127,2048]{1,0:T(8,128)(2,1)S(1)}, bf16[127,2048]{1,0:T(8,128)(2,1)}, u32[]{:S(2)}, u32[]{:S(2)}) collective-permute-start(bf16[127,2048]{1,0:T(8,128)(2,1)S(1)} %bitcast.171), channel_id=1, source_target_pairs={{1,0},{2,1},{3,2},{4,3},{5,4},{6,5},{7,6},{8,7},{9,8},{10,9},{11,1... | collective-permute-start | bytes 1560584 | tf_op jit(solution)/shard_map/ppermute | solution.py:14
  58.5 10.9 %copy-start = (bf16[128,2048]{1,0:T(8,128)(2,1)}, bf16[128,2048]{1,0:T(8,128)(2,1)S(1)}, u32[]{:S(2)}) copy-start(bf16[128,2048]{1,0:T(8,128)(2,1)S(1)} %get-tuple-element.413) | copy-start | bytes 1572868
  58.6 11.6 %collective-permute-start = (bf16[127,2048]{1,0:T(8,128)(2,1)S(1)}, bf16[127,2048]{1,0:T(8,128)(2,1)}, u32[]{:S(2)}, u32[]{:S(2)}) collective-permute-start(bf16[127,2048]{1,0:T(8,128)(2,1)S(1)} %slice.776), channel_id=1, source_target_pairs={{0,1},{1,2},{2,3},{3,4},{4,5},{5,6},{6,7},{7,8},{8,9},{9,10},{10,1... | collective-permute-start | bytes 1560584 | tf_op jit(solution)/shard_map/ppermute | solution.py:14
  116.9 42.6 %copy-start.1 = (bf16[1,128,2048]{2,1,0:T(8,128)(2,1)S(1)}, bf16[1,128,2048]{2,1,0:T(8,128)(2,1)}, u32[]{:S(2)}) copy-start(bf16[1,128,2048]{2,1,0:T(8,128)(2,1)} %param.11) | copy-start | bytes 1572868
  116.9 42.6 %copy-start.2 = (bf16[1,128,2048]{2,1,0:T(8,128)(2,1)S(1)}, bf16[1,128,2048]{2,1,0:T(8,128)(2,1)}, u32[]{:S(2)}) copy-start(bf16[1,128,2048]{2,1,0:T(8,128)(2,1)} %param.14) | copy-start | bytes 1572868
Sparse Core Ops, SparseCore 0:
  117.0 137.1 all-reduce.1
where the time goes:
time: 264 us; the launch traced here: 263 us
  other arithmetic  101 us (38%)
  waiting for transfers between devices  95.8 us (36%)
  local copies, waits for them, and re-layouts  38.6 us (15%)
  between operations  14.2 us (5%)
  starting transfers between devices  12.1 us (5%)
    psum x1, waiting for transfers between devices, per_device(): summed = lax.psum(partial_sum, ('dp', 'ctx'))  93.5 us
    reduce_sum x8, other arithmetic, lag_advance(): jnp.sum(grad_float * window[start_row:start_row + length], axis=0)  34.7 us
    add x8, other arithmetic, forward_advance(): running = running + coeffs[inner] * window[start_row:start_row + length]  27.7 us
    add x8, other arithmetic, backward_advance(): running = running + coeffs[inner] * window[inner:inner + length]  27.2 us
    slice x8, local copies, waits for them, and re-layouts, forward_advance(): running = running + coeffs[inner] * window[start_row:start_row + length]  14.4 us
    slice x8, local copies, waits for them, and re-layouts, backward_advance(): running = running + coeffs[inner] * window[inner:inner + length]  14.4 us
    ppermute x2, starting transfers between devices, from_behind(): return lax.ppermute(array, axis, pairs)  12 us
    dynamic_update_slice x8, local copies, waits for them, and re-layouts, lag_advance(): return lax.dynamic_update_slice_in_dim(running, jnp.stack(lines), first, 0)  5.29 us
  transfers between devices with their start and end apart: 3, of which 3 were waited for; matrix products, arithmetic and copies ran while one was open for 17% of the time, Pallas kernels for 0%

commit v1 on v0

v1 whole, which is shorter than its diff:
```python
import functools
import math

import jax
import jax.numpy as jnp
import ml_dtypes
import numpy as np
from jax import lax
from jax.experimental import pallas as pl
from jax.experimental.pallas import tpu as pltpu
from jax.sharding import PartitionSpec as P

bf16 = jnp.bfloat16
f32 = jnp.float32
small_bytes = 10 * 1024 * 1024
large_bytes = 20 * 1024 * 1024
pieces_inside = 4
tile = 512
lanes = 128
load_rows = 32
near = pl.BlockSpec(memory_space=pltpu.VMEM)
far = pl.BlockSpec(memory_space=pltpu.HBM)


def high_low(matrix):
    high = matrix.astype(ml_dtypes.bfloat16)
    low = (matrix - high.astype(np.float64)).astype(ml_dtypes.bfloat16)
    return high, low


def transforms(size, taps):
    angle = np.pi * (4 * np.arange(size) + 1) / (2 * size)
    phase = angle[:, None] * np.arange(size)[None, :]
    real, imag = np.cos(phase), np.sin(phase)
    one = np.concatenate([real, imag], axis=0)
    upper = np.concatenate([-imag.T, real.T], axis=1) / size
    lower = np.concatenate([real.T, imag.T], axis=1) / size
    lag = (size - np.arange(taps))[:, None] * angle[None, :]
    lags = np.concatenate([np.cos(lag), np.sin(lag)], axis=1) / size
    turned = np.concatenate([imag.T, -real.T], axis=1)[:taps] / size

    def forward(matrix):
        return np.concatenate(high_low(matrix), axis=1)

    def inverse(matrix):
        high, low = high_low(matrix)
        return np.concatenate([high, high, low], axis=1)

    return (
        forward(one[:, :taps]),
        forward(one),
        inverse(upper),
        inverse(lower),
        np.stack([inverse(lags), inverse(turned)]),
    )


def spectrum(matrix, block):
    stacked = jnp.concatenate([block, block], axis=0)
    both = jnp.dot(matrix, stacked, preferred_element_type=f32)
    half = both.shape[0] // 2
    return both[:half], both[half:]


def back(matrix, real, imag):
    both = jnp.concatenate([real, imag], axis=0)
    high = both.astype(bf16)
    low = (both - high.astype(f32)).astype(bf16)
    return jnp.dot(
        matrix, jnp.concatenate([high, low, high], axis=0), preferred_element_type=f32
    )


def times(left, right):
    (lr, li), (rr, ri) = left, right
    return lr * rr - li * ri, lr * ri + li * rr


def times_conjugate(left, right):
    (lr, li), (rr, ri) = left, right
    return lr * rr + li * ri, li * rr - lr * ri


def window(first, second):
    return first[0] - second[1], first[1] + second[0]


def product(left, right):
    return (left.astype(f32) * right.astype(f32)).astype(bf16)


def forward_strip(one, upper, before, kv, weights, query, grad):
    both = window(spectrum(one, before), spectrum(one, kv))
    mixed = back(upper, *times(both, weights))
    return (query.astype(f32) * mixed).astype(bf16), (grad.astype(f32) * mixed).astype(bf16)


def backward_strip(one, lower, gate, beyond, weights, key, value):
    both = window(spectrum(one, gate), spectrum(one, beyond))
    flowing = back(lower, *times_conjugate(both, weights))
    return (flowing * value.astype(f32)).astype(bf16), (flowing * key.astype(f32)).astype(bf16)


def tiles(ref):
    return [slice(at, at + tile) for at in range(0, ref.shape[1], tile)]


def halves(ref):
    size = ref.shape[0] // 2
    return slice(0, size), slice(size, 2 * size)


def core():
    return lax.rem(lax.axis_index("ctx"), 2)


def blocks(parity, number, share):
    first = number * (tile // share)
    return [
        slice((2 * place + parity) * share, (2 * place + parity + 1) * share)
        for place in range(first, first + tile // share)
    ]


def gather(ref, columns):
    return jnp.concatenate([ref[:, cols] for cols in columns], axis=1)


def take(pieces, start, stop):
    width = pieces[0].shape[1]
    return jnp.concatenate(
        [
            pieces[at // width][:, at % width : at % width + lanes]
            for at in range(start, stop, lanes)
        ],
        axis=1,
    )


def wait(copies):
    for copy in copies:
        copy.wait()


def first_kernel(share, query, grad, key, value, out, left, right, sems):
    count = out.shape[1] // share

    def copies(pair, parity):
        return [
            pltpu.make_async_copy(
                source.at[:, (2 * place + parity) * share : (2 * place + parity + 1) * share],
                held.at[:, place * share : (place + 1) * share],
                sems.at[which, place],
            )
            for place in range(count)
            for which, (source, held) in enumerate(zip(pair, (left, right)))
        ]

    for parity, pair in enumerate(((query, grad), (key, value))):

        @pl.when(core() == parity)
        def _():
            for copy in copies(pair, 1 - parity):
                copy.start()

    for place, copy in enumerate(copies((key, value), 0)):
        copy.wait()
        if place % 2:
            cols = slice(place // 2 * share, (place // 2 + 1) * share)
            out[:, cols] = product(left[:, cols], right[:, cols])


def start_loads(sources, held, sems):
    rows = [slice(at, at + load_rows) for at in range(0, held[0].shape[0], load_rows)]
    groups = [
        [
            pltpu.make_async_copy(source.at[part], place.at[part], sems.at[which, number])
            for which, (source, place) in enumerate(zip(sources, held))
        ]
        for number, part in enumerate(rows)
    ]
    for group in groups:
        for copy in group:
            copy.start()
    return rows, groups


def prepare_kernel(share, *refs):
    sources, held, base, sends, sems = refs[:4], refs[5:9], refs[9], refs[10:-1], refs[-1]
    query, grad, key, value = held
    half, width = base.shape[1], sends[0].shape[1]
    rows, groups = start_loads(sources, held, sems)

    def run(parity):
        pairs = (key, value), (query, grad)
        first, second = pairs if parity == 0 else pairs[::-1]
        for part, group in zip(rows, groups):
            wait(group)
            for offset in range(0, half, lanes):
                start = 2 * (offset // share) * share + offset % share
                own = slice(start + parity * share, start + parity * share + lanes)
                other = slice(start + (1 - parity) * share, start + (1 - parity) * share + lanes)

                def put(ref, at, pair, cols):
                    ref[part, at : at + lanes] = product(pair[0][part, cols], pair[1][part, cols])

                put(base, offset, second, own)
                for number, (pair, cols) in enumerate(
                    ((second, other), (first, other), (first, own))
                ):
                    where = number * half + offset
                    put(sends[where // width], where % width, pair, cols)

    for parity in range(2):
        pl.when(core() == parity)(functools.partial(run, parity))


def inside_kernel(one, base, *refs):
    sends, came = refs[:pieces_inside], refs[pieces_inside : 2 * pieces_inside]
    cross, spectra = refs[2 * pieces_inside :]
    sign = 1.0 - 2.0 * core().astype(f32)
    real, imag = halves(cross)
    half = base.shape[1]
    for cols in tiles(base):
        low, high = cols.start, cols.stop
        own_first = spectrum(one[...], take(sends, 2 * half + low, 2 * half + high))
        own_base = spectrum(one[...], base[:, cols])
        other_first = spectrum(one[...], take(came, low, high))
        other_base = spectrum(one[...], take(came, half + low, half + high))
        spectra[real, cols], spectra[imag, cols] = own_base
        ar, ai = times_conjugate(own_first, own_base)
        both = own_first[0] - sign * other_first[1], own_first[1] + sign * other_first[0]
        br, bi = times_conjugate(both, other_base)
        cross[real, cols] = br - sign * ai
        cross[imag, cols] = bi + sign * ar


def divide(totals, sends, level):
    width, below, here = level
    own = lax.rem(lax.div(lax.axis_index("ctx"), 2 * here), width)
    for number, send in enumerate(sends):
        other = jnp.bitwise_xor(own, number)
        for place in range(below):
            send[place] = totals[other * below + place].astype(send.dtype)


def lag_kernel(level, one, lags, halo, cross, spectra, *refs):
    sends, totals = refs[:-1], refs[-1]
    real, imag = halves(cross)
    share = totals.shape[2]
    matrix = lags[core()]
    for cols in tiles(halo):
        ar, ai = times_conjugate(
            spectrum(one[...], halo[:, cols]), (spectra[real, cols], spectra[imag, cols])
        )
        sums = back(matrix, cross[real, cols] + ar, cross[imag, cols] + ai)
        for start in range(0, tile, share):
            totals[(cols.start + start) // share] = sums[:, start : start + share]
    divide(totals, sends, level)


def join_kernel(level, came, keep, *refs):
    arrived, sends, totals = refs[:came], refs[came + 1 : -1], refs[-1]
    for place in range(totals.shape[0]):
        value = keep[place]
        for part in arrived:
            value = value + part[place].astype(f32)
        totals[place] = value
    divide(totals, sends, level)


def total_kernel(scale, *refs):
    parts, (out, held, sem) = refs[:-4], refs[-3:]
    planes = []
    for plane in (parts[: len(parts) // 2], parts[len(parts) // 2 :]):
        value = plane[0][0].astype(f32)
        for part in plane[1:]:
            value = value + part[0].astype(f32)
        planes.append(value)
    held[...] = (planes[0] + planes[1]) * scale
    copy = pltpu.make_async_copy(held, out, sem)
    copy.start()
    copy.wait()


def spread(held, results, columns, share):
    for which, result in enumerate(results):
        for number, cols in enumerate(columns):
            held[which, :, cols] = result[:, number * share : (number + 1) * share]


def send_out(held, outs, cols, sems):
    copies = [
        pltpu.make_async_copy(held.at[which, :, cols], out.at[:, cols], sems.at[which])
        for which, out in enumerate(outs)
    ]
    for copy in copies:
        copy.start()
    return copies


def rows_of(array, count):
    size = array.shape[0] // count
    return [slice(at, at + size) for at in range(0, array.shape[0], size)]


def inside_way_kernel(share, query, key, value, grad, one, *refs):
    fetched, came, refs = refs[:3], refs[3 : 3 + pieces_inside], refs[4 + pieces_inside :]
    held, upper, lower, taps, sems = refs
    half = taps.shape[1] // 2
    fetches = [
        pltpu.make_async_copy(source.at[rows], place.at[rows], sems.at[number, part])
        for number, (source, place) in enumerate(zip(fetched, (upper, lower, taps)))
        for part, rows in enumerate(rows_of(place, sems.shape[1]))
    ]
    for fetch in fetches:
        fetch.start()
    wait(fetches)

    def run(parity):
        for number in range(half // tile):
            for side in (parity, 1 - parity):
                columns = blocks(side, number, share)
                start = (half if side == parity else 2 * half) + number * tile
                halo = take(came, start, start + tile)
                weights = spectrum(one[...], gather(taps, columns))
                around = gather(query, columns), gather(grad, columns)
                within = gather(key, columns), gather(value, columns)
                if parity == 0:
                    results = backward_strip(
                        one[...], lower[...], product(*around), halo, weights, *within
                    )
                else:
                    results = forward_strip(
                        one[...], upper[...], halo, product(*within), weights, *around
                    )
                spread(held, results, columns, share)

    for parity in range(2):
        pl.when(core() == parity)(functools.partial(run, parity))


def across_way(share, late, parity, held, query, key, value, grad, one, upper, lower, taps, halo):
    for number in range(halo.shape[1] // tile):
        packed = slice(number * tile, (number + 1) * tile)
        columns = blocks(1 - parity if late else parity, number, share)
        weights = spectrum(one[...], gather(taps, columns))
        around = gather(query, columns), gather(grad, columns)
        within = gather(key, columns), gather(value, columns)
        if parity == 0:
            results = forward_strip(
                one[...], upper[...], halo[:, packed], product(*within), weights, *around
            )
        else:
            results = backward_strip(
                one[...], lower[...], product(*around), halo[:, packed], weights, *within
            )
        spread(held, results, columns, share)
        yield columns


def across_first_kernel(share, *refs):
    inputs, before, refs = refs[:9], refs[9], refs[11:]
    outs, held, sems = refs[:4], refs[4], refs[5]

    def run(parity):
        inner = outs[2:] if parity == 0 else outs[:2]
        copies = [
            pltpu.make_async_copy(before.at[which, rows], out.at[rows], sems.at[which, part])
            for which, out in enumerate(inner)
            for part, rows in enumerate(rows_of(out, sems.shape[1]))
        ]
        for copy in copies:
            copy.start()
        for _ in across_way(share, False, parity, held, *inputs):
            pass
        wait(copies)

    for parity in range(2):
        pl.when(core() == parity)(functools.partial(run, parity))


def across_late_kernel(share, *refs):
    inputs, before, refs = refs[:9], refs[9], refs[15:]
    outs, held, sems = refs[:4], refs[4], refs[5]

    def run(parity):
        outer = outs[:2] if parity == 0 else outs[2:]
        copies = []
        for number in range(inputs[-1].shape[1] // tile):
            for which, cols in enumerate(blocks(parity, number, share)):
                place = sems.at[0, number * (tile // share) + which]
                copies += send_out(before, outer, cols, place)
        for number, columns in enumerate(across_way(share, True, parity, held, *inputs)):
            for which, cols in enumerate(columns):
                place = sems.at[1, number * len(columns) + which]
                copies += send_out(held, outer, cols, place)
        wait(copies)

    for parity in range(2):
        pl.when(core() == parity)(functools.partial(run, parity))


def plain_load_kernel(*refs):
    query, grad, key, value, kv, gate, sems = refs[4:]
    rows, groups = start_loads(refs[:4], refs[4:8], sems)
    for part, group in zip(rows, groups):
        wait(group)
        kv[part] = product(key[part], value[part])
        gate[part] = product(query[part], grad[part])


def plain_lag_kernel(one, lags, before, kv, gate, sums):
    for cols in tiles(kv):
        both = window(spectrum(one[...], before[:, cols]), spectrum(one[...], kv[:, cols]))
        values = back(lags[0], *times_conjugate(both, spectrum(one[...], gate[:, cols])))
        sums[:, cols] = values.astype(bf16)


def plain_filter_kernel(
    first, one, upper, lower, before, kv, gate, beyond, taps, query, key, value, grad,
    output, grad_query, grad_key, grad_value,
):
    for cols in tiles(kv):
        weights = spectrum(first[...], taps[:, cols])
        output[:, cols], grad_query[:, cols] = forward_strip(
            one[...], upper[...], before[:, cols], kv[:, cols], weights,
            query[:, cols], grad[:, cols],
        )
        grad_key[:, cols], grad_value[:, cols] = backward_strip(
            one[...], lower[...], gate[:, cols], beyond[:, cols], weights,
            key[:, cols], value[:, cols],
        )


def call(
    kernel, name, inputs, outs, scratch=(), far_ins=(), any_ins=(), far_outs=(),
    limit=small_bytes, flops=0, **more
):
    def space(at):
        return pl.ANY if at in any_ins else pltpu.HBM if at in far_ins else pltpu.VMEM

    inputs = [
        pltpu.with_memory_space_constraint(array, space(at)) for at, array in enumerate(inputs)
    ]
    return pl.pallas_call(
        kernel,
        in_specs=[pl.BlockSpec(memory_space=space(at)) for at in range(len(inputs))],
        out_specs=[far if at in far_outs else near for at in range(len(outs))],
        out_shape=[
            (pltpu.HBM if at in far_outs else pltpu.VMEM)(out.shape, out.dtype)
            for at, out in enumerate(outs)
        ],
        scratch_shapes=scratch,
        cost_estimate=pl.CostEstimate(flops=flops, bytes_accessed=0, transcendentals=0),
        compiler_params=pltpu.CompilerParams(vmem_limit_bytes=limit),
        name=name,
        **more,
    )(*inputs)


def shift(array, axis, by):
    devices = lax.axis_size(axis)
    return lax.ppermute(
        array, axis, [(i, i + by) for i in range(devices) if 0 <= i + by < devices]
    )


def sum_over_dp(own):
    dp = lax.axis_size("dp")
    if dp == 1:
        return own
    if dp == 2:
        return own + lax.ppermute(own, "dp", [(0, 1), (1, 0)])
    came = [own] + [
        lax.ppermute(own, "dp", [(i, (i + by) % dp) for i in range(dp)]) for by in range(1, dp)
    ]
    order = lax.rem(lax.axis_index("dp") - jnp.arange(dp) + dp, dp)
    return jnp.sum(jnp.stack(came)[order], axis=0)


def shape(dims, dtype):
    return jax.ShapeDtypeStruct(dims, dtype)


def levels(ctx):
    chips, found = ctx // 2, []
    while chips > 1:
        width = 4 if chips % 4 == 0 else 2
        chips //= width
        found.append((width, chips, chips))
    return found


def paired(query, key, value, grad, filter_taps):
    length, channels = query.shape
    taps = filter_taps.shape[0]
    ctx = lax.axis_size("ctx")
    share = channels // ctx
    half = channels // 2
    _, one, upper, lower, lags = transforms(length, taps)
    block, strip = shape((length, channels), bf16), shape((length, half), bf16)
    spectra = shape((2 * length, half), f32)
    sources = query, grad, key, value
    inside = [(i, i ^ 1) for i in range(ctx)]
    across = [(i, i + 1) for i in range(1, ctx - 1, 2)]
    across += [(i + 1, i) for i, _ in across]

    (urgent,) = call(
        functools.partial(first_kernel, share), "first", sources, [strip],
        far_ins=range(4),
        scratch=[pltpu.VMEM((length, half), bf16)] * 2
        + [pltpu.SemaphoreType.DMA((2, ctx // 2))],
    )
    halo = lax.ppermute(urgent, "ctx", across)
    piece = shape((length, 3 * half // pieces_inside), bf16)
    query, grad, key, value, base, *sends = call(
        functools.partial(prepare_kernel, share), "prepare", (*sources, urgent),
        [block] * 4 + [strip] + [piece] * pieces_inside,
        far_ins=range(4),
        scratch=[pltpu.SemaphoreType.DMA((4, length // load_rows))],
    )
    late = lax.ppermute(base, "ctx", across)
    came = [lax.ppermute(send, "ctx", inside) for send in sends]
    cross, base_spectra = call(
        inside_kernel, "inside", (one, base, *sends, *came), [spectra, spectra]
    )

    def split(level, last):
        width, below, _ = level
        first = shape((below, taps, share), bf16 if last else f32)
        return [first] + [shape((below, taps, share), bf16)] * (width - 1)

    def partner(level, number, over=0):
        step = 2 * level[2] * number
        return [(at, at ^ step ^ over) for at in range(2 * ctx)]

    order = levels(ctx)
    keep, *sends = call(
        functools.partial(lag_kernel, order[0]), "lags",
        (one, lags, halo, cross, base_spectra),
        split(order[0], len(order) == 1),
        scratch=[pltpu.VMEM((ctx // 2, taps, share), f32)],
    )
    held = query, key, value, grad, one
    fetched = upper, lower, filter_taps
    wide = shape((2, length, channels), bf16)
    inner, upper, lower, filter_taps = call(
        functools.partial(inside_way_kernel, share), "inside_way",
        (*held, *fetched, *came, keep),
        [wide] + [shape(array.shape, bf16) for array in fetched],
        far_ins=range(5, 8),
        scratch=[pltpu.SemaphoreType.DMA((len(fetched), 4))],
        limit=large_bytes,
        flops=3 * 10**9,
    )
    held = *held, upper, lower, filter_taps
    *results, outer = call(
        functools.partial(across_first_kernel, share), "across_first",
        (*held, halo, inner, keep),
        [block] * 4 + [wide],
        far_outs=range(4),
        scratch=[pltpu.SemaphoreType.DMA((2, 4))],
        limit=large_bytes,
        flops=3 * 10**9,
    )
    for level, left in zip(order, order[1:]):
        arrived = [
            lax.ppermute(sends[number - 1], ("dp", "ctx"), partner(level, number))
            for number in (*range(2, level[0]), 1)
        ]
        below = level[1]
        keep, *sends = call(
            functools.partial(join_kernel, left, len(arrived)), "join",
            (keep, *arrived, results[0]),
            split(left, left is order[-1]),
            far_ins=(len(arrived) + 1,),
            scratch=[pltpu.VMEM((below, taps, share), f32)],
        )
    parts = [
        lax.ppermute(send, ("dp", "ctx"), partner(order[-1], number, over))
        if number or over
        else send
        for over in (0, ctx)
        for number, send in enumerate([keep] + sends)
    ]
    results = call(
        functools.partial(across_late_kernel, share), "across_late",
        (*held, late, outer, keep, *results),
        [block] * 4,
        far_ins=range(11, 15),
        far_outs=range(4),
        input_output_aliases={11 + at: at for at in range(4)},
        scratch=[
            pltpu.VMEM(wide.shape, bf16),
            pltpu.SemaphoreType.DMA((2, ctx // 2, 2)),
        ],
        limit=large_bytes,
    )
    (total,) = call(
        functools.partial(total_kernel, 1.0 / math.sqrt(2 * length * ctx)), "total",
        (*parts, results[0]),
        [shape((taps, share), f32)],
        far_ins=(len(parts),),
        far_outs=(0,),
        scratch=[pltpu.VMEM((taps, share), f32), pltpu.SemaphoreType.DMA],
    )
    return results, total


def plain(query, key, value, grad, filter_taps):
    length, channels = query.shape
    taps = filter_taps.shape[0]
    ctx = lax.axis_size("ctx")
    share = channels // ctx
    first, one, upper, lower, lags = transforms(length, taps)
    block = shape((length, channels), bf16)
    query, grad, key, value, kv, gate = call(
        plain_load_kernel, "load", (query, grad, key, value), [block] * 6,
        far_ins=range(4),
        scratch=[pltpu.SemaphoreType.DMA((4, length // load_rows))],
    )
    before, beyond = shift(kv, "ctx", 1), shift(gate, "ctx", -1)
    (sums,) = call(
        plain_lag_kernel, "lags", (one, lags, before, kv, gate), [shape((taps, channels), bf16)],
    )
    parts = jnp.transpose(sums.reshape(taps, ctx, share), (1, 0, 2))
    pieces = lax.all_to_all(parts, "ctx", 0, 0, tiled=True)
    total = sum_over_dp(jnp.sum(pieces.astype(f32), axis=0))
    total = total * (1.0 / math.sqrt(length * ctx * lax.axis_size("dp")))
    results = call(
        plain_filter_kernel, "filters",
        (first, one, upper, lower, before, kv, gate, beyond, filter_taps)
        + (query, key, value, grad),
        [block] * 4,
    )
    return results, total


def per_device(query_act, key_act, value_act, grad_out, filter_taps):
    length, channels = query_act.shape[1:]
    ctx, dp = lax.axis_size("ctx"), lax.axis_size("dp")
    share = channels // ctx
    fits = ctx & (ctx - 1) == 0 and ctx > 2 and share % lanes == 0 and tile % share == 0
    fits = fits and filter_taps.shape[0] == length and dp == 2
    run = paired if fits and channels % (2 * tile) == 0 and channels % 1024 == 0 else plain
    results, total = run(query_act[0], key_act[0], value_act[0], grad_out[0], filter_taps)
    return tuple(result[None] for result in results) + (total,)


def solution(mesh):
    sharded = P("dp", "ctx", None)
    return jax.shard_map(
        per_device,
        mesh=mesh,
        in_specs=(sharded, sharded, sharded, sharded, P()),
        out_specs=(sharded, sharded, sharded, sharded, P(None, "ctx")),
        check_vma=False,
    )
```

time: 264 us -> 33.4 us (0.13)
  other arithmetic: 101 us -> 0 us
  waiting for transfers between devices: 95.8 us -> 1.87 us
  local copies, waits for them, and re-layouts: 38.6 us -> 0.01 us
  Pallas kernels: 0 us -> 13.6 us
  between operations: 14.2 us -> 0.79 us
  starting transfers between devices: 12.1 us -> 16.9 us
    psum x1 -> x0, waiting for transfers between devices: 93.5 us -> none  [per_device(): summed = lax.psum(partial_sum, ('dp', 'ctx'))]
    add x16 -> x0, other arithmetic: 54.9 us -> none  [the longest x8 27.7 us: forward_advance(): running = running + coeffs[inner] * window[start_row:start_row + length]]
    reduce_sum x8 -> x0, other arithmetic: 34.7 us -> none  [lag_advance(): jnp.sum(grad_float * window[start_row:start_row + length], axis=0)]
    slice x17 -> x0, local copies, waits for them, and re-layouts: 29 us -> none  [the longest x8 14.4 us: forward_advance(): running = running + coeffs[inner] * window[start_row:start_row + length]]
    pallas_call x0 -> x9, Pallas kernels: none -> 13.6 us  [call(): pl.pallas_call(kernel, in_specs=[pl.BlockSpec(memory_space=space(at)) for...]
    dynamic_update_slice x8 -> x0, local copies, waits for them, and re-layouts: 5.29 us -> none  [lag_advance(): return lax.dynamic_update_slice_in_dim(running, jnp.stack(lines), first, 0)]
    ppermute x2 -> x12, starting transfers between devices: 12 us -> 16.9 us  [the longest x3 6.78 us: paired(): lax.ppermute(sends[number - 1], ('dp', 'ctx'), partner(level, number))]
    broadcast_in_dim x2 -> x0, other arithmetic: 3.76 us -> none  [the longest x1 2.52 us: per_device(): grad_value_rows[None]]
  transfers between devices with their start and end apart: 3 -> 12, of which waited for: 3 -> 4; matrix products, arithmetic and copies ran while one was open for 17% -> 0% of each run, Pallas kernels for 0% -> 35%
where the time goes in v1:
time: 33.4 us; the launch traced here: 33.2 us
  starting transfers between devices  16.9 us (51%)
  Pallas kernels  13.6 us (41%)
  waiting for transfers between devices  1.87 us (6%)
  between operations  0.79 us (2%)
    pallas_call x9, Pallas kernels, call(): pl.pallas_call(kernel, in_specs=[pl.BlockSpec(memory_space=space(at)) for...  13.6 us
    ppermute x3, starting transfers between devices, paired(): lax.ppermute(sends[number - 1], ('dp', 'ctx'), partner(level, number))  6.78 us
    ppermute x4, starting transfers between devices, paired(): came = [lax.ppermute(send, 'ctx', inside) for send in sends]  4.97 us
    ppermute x3, starting transfers between devices, paired(): lax.ppermute(send, ('dp', 'ctx'), partner(order[-1], number, over))  3.55 us
    ppermute x3, waiting for transfers between devices, paired(): lax.ppermute(send, ('dp', 'ctx'), partner(order[-1], number, over))  1.13 us
    ppermute x1, starting transfers between devices, paired(): halo = lax.ppermute(urgent, 'ctx', across)  0.81 us
    ppermute x1, starting transfers between devices, paired(): late = lax.ppermute(base, 'ctx', across)  0.8 us
  transfers between devices with their start and end apart: 12, of which 4 were waited for; matrix products, arithmetic and copies ran while one was open for 0% of the time, Pallas kernels for 35%

profile of v1, /device:TPU:0, one launch (start us, length us, event | category | flops | bytes accessed | tf_op | source)
XLA Modules:
  0.0 33.2 jit_solution(12957810803818083810)
XLA Ops:
  0.6 1.2 %first.1.refs_4_ = bf16[128,1024]{1,0:T(8,128)(2,1)S(1)} custom-call(bf16[128,2048]{1,0:T(8,128)(2,1)} %bitcast.9, bf16[128,2048]{1,0:T(8,128)(2,1)} %bitcast.11, bf16[128,2048]{1,0:T(8,128)(2,1)} %bitcast.13, bf16[128,2048]{1,0:T(8,128)(2,1)} %bitcast.15), custom_call_target="tpu_custom_call" | custom-call | tf_op jit(solution)/shard_map/first/pallas_call | solution.py:446
  1.8 0.0 copy-start
  1.8 0.8 %collective-permute-start.4 = (bf16[128,1024]{1,0:T(8,128)(2,1)S(1)}, bf16[128,1024]{1,0:T(8,128)(2,1)S(1)}, u32[]{:S(2)}, u32[]{:S(2)}) collective-permute-start(bf16[128,1024]{1,0:T(8,128)(2,1)S(1)} %first.1.refs_4_), channel_id=1, source_target_pairs={{1,2},{3,4},{5,6},{7,8},{9,10},{11,12},{13,14},{2,1},{4,3},{6,5},{... | collective-permute-start | bytes 786440 | tf_op jit(solution)/shard_map/ppermute | solution.py:515
  2.7 1.8 %prepare.1 = (bf16[128,2048]{1,0:T(8,128)(2,1)S(1)}, bf16[128,2048]{1,0:T(8,128)(2,1)S(1)}, bf16[128,2048]{1,0:T(8,128)(2,1)S(1)}, bf16[128,2048]{1,0:T(8,128)(2...) custom-call(bf16[128,2048]{1,0:T(8,128)(2,1)} %bitcast.10, ...), custom_call_target="tpu_custom_call" | custom-call | tf_op jit(solution)/shard_map/prepare/pallas_call | solution.py:446
  4.5 4.4 %collective-permute-start = (bf16[128,768]{1,0:T(8,128)(2,1)S(1)}, bf16[128,768]{1,0:T(8,128)(2,1)S(1)}, u32[]{:S(2)}, u32[]{:S(2)}) collective-permute-start(bf16[128,768]{1,0:T(8,128)(2,1)S(1)} %get-tuple-element.39.refs_0_), channel_id=1, source_target_pairs={{0,1},{1,0},{2,3},{3,2},{4,5},{5,4},{6,7},{7,6},{8,9},{9,8},{10,11... | collective-permute-start | bytes 589832 | tf_op jit(solution)/shard_map/ppermute | solution.py:524
  8.9 0.1 collective-permute-start.1
  8.9 0.4 %collective-permute-start.2 = (bf16[128,768]{1,0:T(8,128)(2,1)S(1)}, bf16[128,768]{1,0:T(8,128)(2,1)S(1)}, u32[]{:S(2)}, u32[]{:S(2)}) collective-permute-start(bf16[128,768]{1,0:T(8,128)(2,1)S(1)} %get-tuple-element.41.refs_2_), channel_id=1, source_target_pairs={{0,1},{1,0},{2,3},{3,2},{4,5},{5,4},{6,7},{7,6},{8,9},{9,8},{10,11... | collective-permute-start | bytes 589832 | tf_op jit(solution)/shard_map/ppermute | solution.py:524
  9.4 0.1 collective-permute-start.3
  9.4 0.5 %collective-permute-done.refs_4_.refs_3_ = bf16[128,768]{1,0:T(8,128)(2,1)S(1)} collective-permute-done((bf16[128,768]{1,0:T(8,128)(2,1)S(1)}, bf16[128,768]{1,0:T(8,128)(2,1)S(1)}, u32[]{:S(2)}, u32[]{:S(2)}) %collective-permute-start) | collective-permute-done | bytes 196640 | tf_op jit(solution)/shard_map/ppermute | solution.py:524
  9.9 0.0 copy-start.1
  9.9 0.8 %collective-permute-start.5 = (bf16[128,1024]{1,0:T(8,128)(2,1)S(1)}, bf16[128,1024]{1,0:T(8,128)(2,1)S(1)}, u32[]{:S(2)}, u32[]{:S(2)}) collective-permute-start(bf16[128,1024]{1,0:T(8,128)(2,1)S(1)} %get-tuple-element.43.base), channel_id=1, source_target_pairs={{1,2},{3,4},{5,6},{7,8},{9,10},{11,12},{13,14},{2,1},{4,3},{6,5},{... | collective-permute-start | bytes 786440 | tf_op jit(solution)/shard_map/ppermute | solution.py:523
  10.7 0.0 collective-permute-done.1.refs_5_.refs_4_
  10.7 0.0 collective-permute-done.2.refs_6_.refs_5_
  10.8 0.1 collective-permute-done.3.refs_7_.refs_6_
  10.9 0.0 copy-done
  10.9 1.0 %inside.1 = (f32[256,1024]{1,0:T(8,128)S(1)}, f32[256,1024]{1,0:T(8,128)S(1)}) custom-call(bf16[256,256]{1,0:T(8,128)(2,1)S(1)} %copy-done, bf16[128,1024]{1,0:T(8,128)(2,1)S(1)} %get-tuple-element.43.base, bf16[128,768]{1,0:T(8,128)(2,1)S(1)} %get-tuple-element.39.refs_0_, bf16[128,768]{1,0:T(8,128)(2,1)S(1)} %get-tuple-element.40.refs_1_, ...), custom_call_target="tpu_custom_call" | custom-call | tf_op jit(solution)/shard_map/inside/pallas_call | solution.py:446
  11.8 0.0 collective-permute-done.4.halo.refs_8_
  11.8 0.0 copy-done.1
  11.8 1.0 %lags.2 = (f32[2,128,128]{2,1,0:T(8,128)S(1)}, bf16[2,128,128]{2,1,0:T(8,128)(2,1)S(1)}, bf16[2,128,128]{2,1,0:T(8,128)(2,1)S(1)}, bf16[2,128,128]{2,1,0:T(8,128)(2,1)S(1)}) custom-call(bf16[256,256]{1,0:T(8,128)(2,1)S(1)} %copy-done, bf16[2,128,768]{2,1,0:T(8,128)(2,1)S(1)} %copy-done.1, bf16[128,1024]{1,0:T(8,128)(2,1)S(1)} %collective-permute-done.4.halo.refs_8_, ...), custom_call_target="tpu_custom_call" | custom-call | tf_op jit(solution)/shard_map/lags/pallas_call | solution.py:446
  12.8 5.2 %collective-permute-start.6 = (bf16[2,128,128]{2,1,0:T(8,128)(2,1)S(1)}, bf16[2,128,128]{2,1,0:T(8,128)(2,1)S(1)}, u32[]{:S(2)}, u32[]{:S(2)}) collective-permute-start(bf16[2,128,128]{2,1,0:T(8,128)(2,1)S(1)} %get-tuple-element.52), channel_id=1, source_target_pairs={{0,8},{1,9},{2,10},{3,11},{4,12},{5,13},{6,14},{7,15},{8,0},{9,1},... | collective-permute-start | bytes 196616 | tf_op jit(solution)/shard_map/ppermute | solution.py:569
  18.0 1.3 %collective-permute-start.7 = (bf16[2,128,128]{2,1,0:T(8,128)(2,1)S(1)}, bf16[2,128,128]{2,1,0:T(8,128)(2,1)S(1)}, u32[]{:S(2)}, u32[]{:S(2)}) collective-permute-start(bf16[2,128,128]{2,1,0:T(8,128)(2,1)S(1)} %get-tuple-element.53), channel_id=1, source_target_pairs={{0,12},{1,13},{2,14},{3,15},{4,8},{5,9},{6,10},{7,11},{8,4},{9,5},... | collective-permute-start | bytes 196616 | tf_op jit(solution)/shard_map/ppermute | solution.py:569
  19.4 0.2 collective-permute-start.8
  19.6 3.7 %inside_way.1 = (bf16[2,128,2048]{2,1,0:T(8,128)(2,1)S(1)}, bf16[128,768]{1,0:T(8,128)(2,1)S(1)}, bf16[128,768]{1,0:T(8,128)(2,1)S(1)}, bf16[128,2048]{1,0:T(8,128)(2,1)S(1)}) custom-call(bf16[128,2048]{1,0:T(8,128)(2,1)S(1)} %get-tuple-element.35.query.refs_0_, bf16[128,2048]{1,0:T(8,128)(2,1)S(1)} %get-tuple-element.36.key.refs_1_, ...), custom_call_target="tpu_custom_call" | custom-call | flops 3000000000 | tf_op jit(solution)/shard_map/inside_way/pallas_call | solution.py:446
  23.3 2.1 %across_first.1 = (bf16[128,2048]{1,0:T(8,128)(2,1)}, bf16[128,2048]{1,0:T(8,128)(2,1)}, bf16[128,2048]{1,0:T(8,128)(2,1)}, bf16[128,2048]{1,0:T(8,128)(2,1)}, bf16[2,128,2048]{2,1,0:T(8,128)(2,1)S(1)}) custom-call(bf16[128,2048]{1,0:T(8,128)(2,1)S(1)} %get-tuple-element.35.query.refs_0_, bf16[128,2048]{1,0:T(8,128)(2,1)S(1)} %get-tuple-element.36.key.refs_1_, ...), custom_call_target="tpu_custom_call" | custom-call | flops 3000000000 | tf_op jit(solution)/shard_map/across_first/pallas_call | solution.py:446
  25.4 0.0 collective-permute-done.6.refs_0_
  25.4 0.0 collective-permute-done.7.refs_1_
  25.4 0.1 collective-permute-done.8.refs_2_
  25.6 1.8 %collective-permute-start.11 = (bf16[1,128,128]{2,1,0:T(8,128)(2,1)S(1)}, bf16[1,128,128]{2,1,0:T(8,128)(2,1)S(1)}, u32[]{:S(2)}, u32[]{:S(2)}) collective-permute-start(bf16[1,128,128]{2,1,0:T(8,128)(2,1)S(1)} %get-tuple-element.64), channel_id=1, source_target_pairs={{0,18},{1,19},{2,16},{3,17},{4,22},{5,23},{6,20},{7,21},{8,26},{9,... | collective-permute-start | bytes 98312 | tf_op jit(solution)/shard_map/ppermute | solution.py:581
  27.3 1.3 %collective-permute-start.9 = (bf16[1,128,128]{2,1,0:T(8,128)(2,1)S(1)}, bf16[1,128,128]{2,1,0:T(8,128)(2,1)S(1)}, u32[]{:S(2)}, u32[]{:S(2)}) collective-permute-start(bf16[1,128,128]{2,1,0:T(8,128)(2,1)S(1)} %get-tuple-element.64), channel_id=1, source_target_pairs={{0,2},{1,3},{2,0},{3,1},{4,6},{5,7},{6,4},{7,5},{8,10},{9,11},{10,... | collective-permute-start | bytes 98312 | tf_op jit(solution)/shard_map/ppermute | solution.py:581
  28.6 0.5 %collective-permute-start.10 = (bf16[1,128,128]{2,1,0:T(8,128)(2,1)S(1)}, bf16[1,128,128]{2,1,0:T(8,128)(2,1)S(1)}, u32[]{:S(2)}, u32[]{:S(2)}) collective-permute-start(bf16[1,128,128]{2,1,0:T(8,128)(2,1)S(1)} %get-tuple-element.56.refs_10_.refs_0_), channel_id=1, source_target_pairs={{0,16},{1,17},{2,18},{3,19},{4,20},{5,21},{6,22},{7,23},{8,24},{9,... | collective-permute-start | bytes 98312 | tf_op jit(solution)/shard_map/ppermute | solution.py:581
  29.1 0.0 collective-permute-done.5.refs_8_
  29.1 2.2 %across_late.1 = (bf16[128,2048]{1,0:T(8,128)(2,1)}, bf16[128,2048]{1,0:T(8,128)(2,1)}, bf16[128,2048]{1,0:T(8,128)(2,1)}, bf16[128,2048]{1,0:T(8,128)(2,1)}) custom-call(bf16[128,2048]{1,0:T(8,128)(2,1)S(1)} %get-tuple-element.35.query.refs_0_, ...), custom_call_target="tpu_custom_call", output_to_operand_aliasing={{0}: (11, {}), {1}: (12, {}), {2}: (13, {}), {3}: (14, {})} | custom-call | tf_op jit(solution)/shard_map/across_late/pallas_call | solution.py:446
  31.4 0.0 collective-permute-done.11.refs_3_
  31.4 0.0 collective-permute-done.9.refs_1_
  31.4 1.1 %collective-permute-done.10.refs_2_ = bf16[1,128,128]{2,1,0:T(8,128)(2,1)S(1)} collective-permute-done((bf16[1,128,128]{2,1,0:T(8,128)(2,1)S(1)}, bf16[1,128,128]{2,1,0:T(8,128)(2,1)S(1)}, u32[]{:S(2)}, u32[]{:S(2)}) %collective-permute-start.10) | collective-permute-done | bytes 32800 | tf_op jit(solution)/shard_map/ppermute | solution.py:581
  32.5 0.7 %total.1 = f32[128,128]{1,0:T(8,128)} custom-call(bf16[1,128,128]{2,1,0:T(8,128)(2,1)S(1)} %get-tuple-element.56.refs_10_.refs_0_, bf16[1,128,128]{2,1,0:T(8,128)(2,1)S(1)} %collective-permute-done.9.refs_1_, bf16[1,128,128]{2,1,0:T(8,128)(2,1)S(1)} %collective-permute-done.10.refs_2_, bf16[1,128,128]{2,1,0:T(8,128)(2,1)S(1)} %collective-permute-done.11.refs_3_, ...), custom_call_target="tpu_custom_call" | custom-call | tf_op jit(solution)/shard_map/total/pallas_call | solution.py:446
  (1 shorter events, 0.0 us)
Async XLA Ops:
  1.8 9.0 %copy-start = (bf16[256,256]{1,0:T(8,128)(2,1)S(1)}, bf16[256,256]{1,0:T(8,128)(2,1)}, u32[]{:S(2)}) copy-start(bf16[256,256]{1,0:T(8,128)(2,1)} %constant.8.clone.one.refs_4_) | copy-start | bytes 393220
  1.8 10.0 %collective-permute-start.4 = (bf16[128,1024]{1,0:T(8,128)(2,1)S(1)}, bf16[128,1024]{1,0:T(8,128)(2,1)S(1)}, u32[]{:S(2)}, u32[]{:S(2)}) collective-permute-start(bf16[128,1024]{1,0:T(8,128)(2,1)S(1)} %first.1.refs_4_), channel_id=1, source_target_pairs={{1,2},{3,4},{5,6},{7,8},{9,10},{11,12},{13,14},{2,1},{4,3},{6,5},{... | collective-permute-start | bytes 786440 | tf_op jit(solution)/shard_map/ppermute | solution.py:515
  4.5 5.4 %collective-permute-start = (bf16[128,768]{1,0:T(8,128)(2,1)S(1)}, bf16[128,768]{1,0:T(8,128)(2,1)S(1)}, u32[]{:S(2)}, u32[]{:S(2)}) collective-permute-start(bf16[128,768]{1,0:T(8,128)(2,1)S(1)} %get-tuple-element.39.refs_0_), channel_id=1, source_target_pairs={{0,1},{1,0},{2,3},{3,2},{4,5},{5,4},{6,7},{7,6},{8,9},{9,8},{10,11... | collective-permute-start | bytes 589832 | tf_op jit(solution)/shard_map/ppermute | solution.py:524
  8.9 1.9 %collective-permute-start.1 = (bf16[128,768]{1,0:T(8,128)(2,1)S(1)}, bf16[128,768]{1,0:T(8,128)(2,1)S(1)}, u32[]{:S(2)}, u32[]{:S(2)}) collective-permute-start(bf16[128,768]{1,0:T(8,128)(2,1)S(1)} %get-tuple-element.40.refs_1_), channel_id=1, source_target_pairs={{0,1},{1,0},{2,3},{3,2},{4,5},{5,4},{6,7},{7,6},{8,9},{9,8},{10,11... | collective-permute-start | bytes 589832 | tf_op jit(solution)/shard_map/ppermute | solution.py:524
  8.9 1.8 %collective-permute-start.2 = (bf16[128,768]{1,0:T(8,128)(2,1)S(1)}, bf16[128,768]{1,0:T(8,128)(2,1)S(1)}, u32[]{:S(2)}, u32[]{:S(2)}) collective-permute-start(bf16[128,768]{1,0:T(8,128)(2,1)S(1)} %get-tuple-element.41.refs_2_), channel_id=1, source_target_pairs={{0,1},{1,0},{2,3},{3,2},{4,5},{5,4},{6,7},{7,6},{8,9},{9,8},{10,11... | collective-permute-start | bytes 589832 | tf_op jit(solution)/shard_map/ppermute | solution.py:524
  9.4 1.5 %collective-permute-start.3 = (bf16[128,768]{1,0:T(8,128)(2,1)S(1)}, bf16[128,768]{1,0:T(8,128)(2,1)S(1)}, u32[]{:S(2)}, u32[]{:S(2)}) collective-permute-start(bf16[128,768]{1,0:T(8,128)(2,1)S(1)} %get-tuple-element.42.refs_3_), channel_id=1, source_target_pairs={{0,1},{1,0},{2,3},{3,2},{4,5},{5,4},{6,7},{7,6},{8,9},{9,8},{10,11... | collective-permute-start | bytes 589832 | tf_op jit(solution)/shard_map/ppermute | solution.py:524
  9.9 1.9 %copy-start.1 = (bf16[2,128,768]{2,1,0:T(8,128)(2,1)S(1)}, bf16[2,128,768]{2,1,0:T(8,128)(2,1)}, u32[]{:S(2)}) copy-start(bf16[2,128,768]{2,1,0:T(8,128)(2,1)} %constant.9.clone.lags) | copy-start | bytes 1179652
  9.9 19.2 %collective-permute-start.5 = (bf16[128,1024]{1,0:T(8,128)(2,1)S(1)}, bf16[128,1024]{1,0:T(8,128)(2,1)S(1)}, u32[]{:S(2)}, u32[]{:S(2)}) collective-permute-start(bf16[128,1024]{1,0:T(8,128)(2,1)S(1)} %get-tuple-element.43.base), channel_id=1, source_target_pairs={{1,2},{3,4},{5,6},{7,8},{9,10},{11,12},{13,14},{2,1},{4,3},{6,5},{... | collective-permute-start | bytes 786440 | tf_op jit(solution)/shard_map/ppermute | solution.py:523
  12.8 12.5 %collective-permute-start.6 = (bf16[2,128,128]{2,1,0:T(8,128)(2,1)S(1)}, bf16[2,128,128]{2,1,0:T(8,128)(2,1)S(1)}, u32[]{:S(2)}, u32[]{:S(2)}) collective-permute-start(bf16[2,128,128]{2,1,0:T(8,128)(2,1)S(1)} %get-tuple-element.52), channel_id=1, source_target_pairs={{0,8},{1,9},{2,10},{3,11},{4,12},{5,13},{6,14},{7,15},{8,0},{9,1},... | collective-permute-start | bytes 196616 | tf_op jit(solution)/shard_map/ppermute | solution.py:569
  18.0 7.4 %collective-permute-start.7 = (bf16[2,128,128]{2,1,0:T(8,128)(2,1)S(1)}, bf16[2,128,128]{2,1,0:T(8,128)(2,1)S(1)}, u32[]{:S(2)}, u32[]{:S(2)}) collective-permute-start(bf16[2,128,128]{2,1,0:T(8,128)(2,1)S(1)} %get-tuple-element.53), channel_id=1, source_target_pairs={{0,12},{1,13},{2,14},{3,15},{4,8},{5,9},{6,10},{7,11},{8,4},{9,5},... | collective-permute-start | bytes 196616 | tf_op jit(solution)/shard_map/ppermute | solution.py:569
  19.4 6.2 %collective-permute-start.8 = (bf16[2,128,128]{2,1,0:T(8,128)(2,1)S(1)}, bf16[2,128,128]{2,1,0:T(8,128)(2,1)S(1)}, u32[]{:S(2)}, u32[]{:S(2)}) collective-permute-start(bf16[2,128,128]{2,1,0:T(8,128)(2,1)S(1)} %get-tuple-element.54), channel_id=1, source_target_pairs={{0,4},{1,5},{2,6},{3,7},{4,0},{5,1},{6,2},{7,3},{8,12},{9,13},{10,... | collective-permute-start | bytes 196616 | tf_op jit(solution)/shard_map/ppermute | solution.py:569
  25.6 5.8 %collective-permute-start.11 = (bf16[1,128,128]{2,1,0:T(8,128)(2,1)S(1)}, bf16[1,128,128]{2,1,0:T(8,128)(2,1)S(1)}, u32[]{:S(2)}, u32[]{:S(2)}) collective-permute-start(bf16[1,128,128]{2,1,0:T(8,128)(2,1)S(1)} %get-tuple-element.64), channel_id=1, source_target_pairs={{0,18},{1,19},{2,16},{3,17},{4,22},{5,23},{6,20},{7,21},{8,26},{9,... | collective-permute-start | bytes 98312 | tf_op jit(solution)/shard_map/ppermute | solution.py:581
  27.3 4.0 %collective-permute-start.9 = (bf16[1,128,128]{2,1,0:T(8,128)(2,1)S(1)}, bf16[1,128,128]{2,1,0:T(8,128)(2,1)S(1)}, u32[]{:S(2)}, u32[]{:S(2)}) collective-permute-start(bf16[1,128,128]{2,1,0:T(8,128)(2,1)S(1)} %get-tuple-element.64), channel_id=1, source_target_pairs={{0,2},{1,3},{2,0},{3,1},{4,6},{5,7},{6,4},{7,5},{8,10},{9,11},{10,... | collective-permute-start | bytes 98312 | tf_op jit(solution)/shard_map/ppermute | solution.py:581
  28.6 3.9 %collective-permute-start.10 = (bf16[1,128,128]{2,1,0:T(8,128)(2,1)S(1)}, bf16[1,128,128]{2,1,0:T(8,128)(2,1)S(1)}, u32[]{:S(2)}, u32[]{:S(2)}) collective-permute-start(bf16[1,128,128]{2,1,0:T(8,128)(2,1)S(1)} %get-tuple-element.56.refs_10_.refs_0_), channel_id=1, source_target_pairs={{0,16},{1,17},{2,18},{3,19},{4,20},{5,21},{6,22},{7,23},{8,24},{9,... | collective-permute-start | bytes 98312 | tf_op jit(solution)/shard_map/ppermute | solution.py:581

commit v2 on v1

--- a/solution.py
+++ b/solution.py
@@ -33,6 +33,7 @@
     phase = angle[:, None] * np.arange(size)[None, :]
     real, imag = np.cos(phase), np.sin(phase)
     one = np.concatenate([real, imag], axis=0)
+    pair = np.concatenate([one, np.concatenate([-imag, real], axis=0)], axis=1)
     upper = np.concatenate([-imag.T, real.T], axis=1) / size
     lower = np.concatenate([real.T, imag.T], axis=1) / size
     lag = (size - np.arange(taps))[:, None] * angle[None, :]
@@ -49,14 +50,15 @@
     return (
         forward(one[:, :taps]),
         forward(one),
+        forward(pair),
         inverse(upper),
         inverse(lower),
         np.stack([inverse(lags), inverse(turned)]),
     )
 
 
-def spectrum(matrix, block):
-    stacked = jnp.concatenate([block, block], axis=0)
+def spectrum(matrix, *blocks):
+    stacked = jnp.concatenate(blocks + blocks, axis=0)
     both = jnp.dot(matrix, stacked, preferred_element_type=f32)
     half = both.shape[0] // 2
     return both[:half], both[half:]
@@ -81,23 +83,17 @@
     return lr * rr + li * ri, li * rr - lr * ri
 
 
-def window(first, second):
-    return first[0] - second[1], first[1] + second[0]
-
-
 def product(left, right):
     return (left.astype(f32) * right.astype(f32)).astype(bf16)
 
 
-def forward_strip(one, upper, before, kv, weights, query, grad):
-    both = window(spectrum(one, before), spectrum(one, kv))
-    mixed = back(upper, *times(both, weights))
+def forward_strip(pair, upper, before, kv, weights, query, grad):
+    mixed = back(upper, *times(spectrum(pair, before, kv), weights))
     return (query.astype(f32) * mixed).astype(bf16), (grad.astype(f32) * mixed).astype(bf16)
 
 
-def backward_strip(one, lower, gate, beyond, weights, key, value):
-    both = window(spectrum(one, gate), spectrum(one, beyond))
-    flowing = back(lower, *times_conjugate(both, weights))
+def backward_strip(pair, lower, gate, beyond, weights, key, value):
+    flowing = back(lower, *times_conjugate(spectrum(pair, gate, beyond), weights))
     return (flowing * value.astype(f32)).astype(bf16), (flowing * key.astype(f32)).astype(bf16)
 
 
@@ -114,12 +110,21 @@
     return lax.rem(lax.axis_index("ctx"), 2)
 
 
+def column_tiles(ref, body):
+    def step(number, carry):
+        body(number, pl.ds(pl.multiple_of(number * tile, tile), tile))
+        return carry
+
+    lax.fori_loop(0, ref.shape[-1] // tile, step, 0)
+
+
 def blocks(parity, number, share):
-    first = number * (tile // share)
-    return [
-        slice((2 * place + parity) * share, (2 * place + parity + 1) * share)
-        for place in range(first, first + tile // share)
+    starts = [
+        2 * number * tile + (2 * place + parity) * share for place in range(tile // share)
     ]
+    if isinstance(number, int):
+        return [slice(start, start + share) for start in starts]
+    return [pl.ds(pl.multiple_of(start, lanes), share) for start in starts]
 
 
 def gather(ref, columns):
@@ -244,6 +249,11 @@
             send[place] = totals[other * below + place].astype(send.dtype)
 
 
+def rows_of(array, count):
+    size = array.shape[0] // count
+    return [slice(at, at + size) for at in range(0, array.shape[0], size)]
+
+
 def lag_kernel(level, one, lags, halo, cross, spectra, *refs):
     sends, totals = refs[:-1], refs[-1]
     real, imag = halves(cross)
@@ -289,28 +299,14 @@
             held[which, :, cols] = result[:, number * share : (number + 1) * share]
 
 
-def send_out(held, outs, cols, sems):
-    copies = [
-        pltpu.make_async_copy(held.at[which, :, cols], out.at[:, cols], sems.at[which])
-        for which, out in enumerate(outs)
-    ]
-    for copy in copies:
-        copy.start()
-    return copies
-
-
-def rows_of(array, count):
-    size = array.shape[0] // count
-    return [slice(at, at + size) for at in range(0, array.shape[0], size)]
-
-
 def inside_way_kernel(share, query, key, value, grad, one, *refs):
-    fetched, came, refs = refs[:3], refs[3 : 3 + pieces_inside], refs[4 + pieces_inside :]
-    held, upper, lower, taps, sems = refs
+    fetched, came, refs = refs[:4], refs[4 : 4 + pieces_inside], refs[5 + pieces_inside :]
+    held, *placed, sems = refs
+    pair, upper, lower, taps = placed
     half = taps.shape[1] // 2
     fetches = [
         pltpu.make_async_copy(source.at[rows], place.at[rows], sems.at[number, part])
-        for number, (source, place) in enumerate(zip(fetched, (upper, lower, taps)))
+        for number, (source, place) in enumerate(zip(fetched, placed))
         for part, rows in enumerate(rows_of(place, sems.shape[1]))
     ]
     for fetch in fetches:
@@ -328,11 +324,11 @@
                 within = gather(key, columns), gather(value, columns)
                 if parity == 0:
                     results = backward_strip(
-                        one[...], lower[...], product(*around), halo, weights, *within
+                        pair[...], lower[...], product(*around), halo, weights, *within
                     )
                 else:
                     results = forward_strip(
-                        one[...], upper[...], halo, product(*within), weights, *around
+                        pair[...], upper[...], halo, product(*within), weights, *around
                     )
                 spread(held, results, columns, share)
 
@@ -340,27 +336,30 @@
         pl.when(core() == parity)(functools.partial(run, parity))
 
 
-def across_way(share, late, parity, held, query, key, value, grad, one, upper, lower, taps, halo):
-    for number in range(halo.shape[1] // tile):
-        packed = slice(number * tile, (number + 1) * tile)
+def across_way(share, late, parity, held, after, *refs):
+    query, key, value, grad, one, pair, upper, lower, taps, halo = refs
+
+    def body(number, packed):
         columns = blocks(1 - parity if late else parity, number, share)
         weights = spectrum(one[...], gather(taps, columns))
         around = gather(query, columns), gather(grad, columns)
         within = gather(key, columns), gather(value, columns)
         if parity == 0:
             results = forward_strip(
-                one[...], upper[...], halo[:, packed], product(*within), weights, *around
+                pair[...], upper[...], halo[:, packed], product(*within), weights, *around
             )
         else:
             results = backward_strip(
-                one[...], lower[...], product(*around), halo[:, packed], weights, *within
+                pair[...], lower[...], product(*around), halo[:, packed], weights, *within
             )
         spread(held, results, columns, share)
-        yield columns
+        after(number)
+
+    column_tiles(halo, body)
 
 
 def across_first_kernel(share, *refs):
-    inputs, before, refs = refs[:9], refs[9], refs[11:]
+    inputs, before, refs = refs[:10], refs[10], refs[12:]
     outs, held, sems = refs[:4], refs[4], refs[5]
 
     def run(parity):
@@ -372,8 +371,7 @@
         ]
         for copy in copies:
             copy.start()
-        for _ in across_way(share, False, parity, held, *inputs):
-            pass
+        across_way(share, False, parity, held, lambda number: None, *inputs)
         wait(copies)
 
     for parity in range(2):
@@ -381,21 +379,29 @@
 
 
 def across_late_kernel(share, *refs):
-    inputs, before, refs = refs[:9], refs[9], refs[15:]
+    inputs, refs = refs[:10], refs[16:]
     outs, held, sems = refs[:4], refs[4], refs[5]
 
     def run(parity):
         outer = outs[:2] if parity == 0 else outs[2:]
-        copies = []
+
+        def copies(number):
+            cols = pl.ds(pl.multiple_of(2 * number * tile, lanes), 2 * tile)
+            return [
+                pltpu.make_async_copy(
+                    held.at[which, rows, cols], out.at[rows, cols], sems.at[number, which, part]
+                )
+                for which, out in enumerate(outer)
+                for part, rows in enumerate(rows_of(out, sems.shape[2]))
+            ]
+
+        def start(number):
+            for copy in copies(number):
+                copy.start()
+
+        across_way(share, True, parity, held, start, *inputs)
         for number in range(inputs[-1].shape[1] // tile):
-            for which, cols in enumerate(blocks(parity, number, share)):
-                place = sems.at[0, number * (tile // share) + which]
-                copies += send_out(before, outer, cols, place)
-        for number, columns in enumerate(across_way(share, True, parity, held, *inputs)):
-            for which, cols in enumerate(columns):
-                place = sems.at[1, number * len(columns) + which]
-                copies += send_out(held, outer, cols, place)
-        wait(copies)
+            wait(copies(number))
 
     for parity in range(2):
         pl.when(core() == parity)(functools.partial(run, parity))
@@ -410,25 +416,25 @@
         gate[part] = product(query[part], grad[part])
 
 
-def plain_lag_kernel(one, lags, before, kv, gate, sums):
+def plain_lag_kernel(one, pair, lags, before, kv, gate, sums):
     for cols in tiles(kv):
-        both = window(spectrum(one[...], before[:, cols]), spectrum(one[...], kv[:, cols]))
+        both = spectrum(pair[...], before[:, cols], kv[:, cols])
         values = back(lags[0], *times_conjugate(both, spectrum(one[...], gate[:, cols])))
         sums[:, cols] = values.astype(bf16)
 
 
 def plain_filter_kernel(
-    first, one, upper, lower, before, kv, gate, beyond, taps, query, key, value, grad,
+    first, pair, upper, lower, before, kv, gate, beyond, taps, query, key, value, grad,
     output, grad_query, grad_key, grad_value,
 ):
     for cols in tiles(kv):
         weights = spectrum(first[...], taps[:, cols])
         output[:, cols], grad_query[:, cols] = forward_strip(
-            one[...], upper[...], before[:, cols], kv[:, cols], weights,
+            pair[...], upper[...], before[:, cols], kv[:, cols], weights,
             query[:, cols], grad[:, cols],
         )
         grad_key[:, cols], grad_value[:, cols] = backward_strip(
-            one[...], lower[...], gate[:, cols], beyond[:, cols], weights,
+            pair[...], lower[...], gate[:, cols], beyond[:, cols], weights,
             key[:, cols], value[:, cols],
         )
 
@@ -498,7 +504,7 @@
     ctx = lax.axis_size("ctx")
     share = channels // ctx
     half = channels // 2
-    _, one, upper, lower, lags = transforms(length, taps)
+    _, one, pair, upper, lower, lags = transforms(length, taps)
     block, strip = shape((length, channels), bf16), shape((length, half), bf16)
     spectra = shape((2 * length, half), f32)
     sources = query, grad, key, value
@@ -543,18 +549,18 @@
         scratch=[pltpu.VMEM((ctx // 2, taps, share), f32)],
     )
     held = query, key, value, grad, one
-    fetched = upper, lower, filter_taps
+    fetched = pair, upper, lower, filter_taps
     wide = shape((2, length, channels), bf16)
-    inner, upper, lower, filter_taps = call(
+    inner, *fetched = call(
         functools.partial(inside_way_kernel, share), "inside_way",
         (*held, *fetched, *came, keep),
         [wide] + [shape(array.shape, bf16) for array in fetched],
-        far_ins=range(5, 8),
+        far_ins=range(5, 9),
         scratch=[pltpu.SemaphoreType.DMA((len(fetched), 4))],
         limit=large_bytes,
         flops=3 * 10**9,
     )
-    held = *held, upper, lower, filter_taps
+    held = *held, *fetched
     *results, outer = call(
         functools.partial(across_first_kernel, share), "across_first",
         (*held, halo, inner, keep),
@@ -584,17 +590,14 @@
         for over in (0, ctx)
         for number, send in enumerate([keep] + sends)
     ]
-    results = call(
+    *results, _ = call(
         functools.partial(across_late_kernel, share), "across_late",
-        (*held, late, outer, keep, *results),
-        [block] * 4,
+        (*held, late, keep, *results, outer),
+        [block] * 4 + [wide],
         far_ins=range(11, 15),
         far_outs=range(4),
-        input_output_aliases={11 + at: at for at in range(4)},
-        scratch=[
-            pltpu.VMEM(wide.shape, bf16),
-            pltpu.SemaphoreType.DMA((2, ctx // 2, 2)),
-        ],
+        input_output_aliases={11 + at: at for at in range(5)},
+        scratch=[pltpu.SemaphoreType.DMA((half // tile, 2, 2))],
         limit=large_bytes,
     )
     (total,) = call(
@@ -613,7 +616,7 @@
     taps = filter_taps.shape[0]
     ctx = lax.axis_size("ctx")
     share = channels // ctx
-    first, one, upper, lower, lags = transforms(length, taps)
+    first, one, pair, upper, lower, lags = transforms(length, taps)
     block = shape((length, channels), bf16)
     query, grad, key, value, kv, gate = call(
         plain_load_kernel, "load", (query, grad, key, value), [block] * 6,
@@ -622,7 +625,7 @@
     )
     before, beyond = shift(kv, "ctx", 1), shift(gate, "ctx", -1)
     (sums,) = call(
-        plain_lag_kernel, "lags", (one, lags, before, kv, gate), [shape((taps, channels), bf16)],
+        plain_lag_kernel, "lags", (one, pair, lags, before, kv, gate), [shape((taps, channels), bf16)],
     )
     parts = jnp.transpose(sums.reshape(taps, ctx, share), (1, 0, 2))
     pieces = lax.all_to_all(parts, "ctx", 0, 0, tiled=True)
@@ -630,7 +633,7 @@
     total = total * (1.0 / math.sqrt(length * ctx * lax.axis_size("dp")))
     results = call(
         plain_filter_kernel, "filters",
-        (first, one, upper, lower, before, kv, gate, beyond, filter_taps)
+        (first, pair, upper, lower, before, kv, gate, beyond, filter_taps)
         + (query, key, value, grad),
         [block] * 4,
     )

time: 33.4 us -> 33.4 us (level)
    ppermute x3, waiting for transfers between devices: 0.14 us -> 0.48 us  [paired(): lax.ppermute(sends[number - 1], ('dp', 'ctx'), partner(level, number))]
  transfers between devices with their start and end apart: 12 -> 12, of which waited for: 4 -> 5; matrix products, arithmetic and copies ran while one was open for 0% -> 0% of each run, Pallas kernels for 35% -> 35%
where the time goes in v2:
time: 33.4 us; the launch traced here: 33.2 us
  starting transfers between devices  16.9 us (51%)
  Pallas kernels  13.5 us (40%)
  waiting for transfers between devices  2.01 us (6%)
  between operations  0.77 us (2%)
    pallas_call x9, Pallas kernels, call(): pl.pallas_call(kernel, in_specs=[pl.BlockSpec(memory_space=space(at)) for...  13.5 us
    ppermute x3, starting transfers between devices, paired(): lax.ppermute(sends[number - 1], ('dp', 'ctx'), partner(level, number))  6.78 us
    ppermute x4, starting transfers between devices, paired(): came = [lax.ppermute(send, 'ctx', inside) for send in sends]  4.97 us
    ppermute x3, starting transfers between devices, paired(): lax.ppermute(send, ('dp', 'ctx'), partner(order[-1], number, over))  3.55 us
    ppermute x3, waiting for transfers between devices, paired(): lax.ppermute(send, ('dp', 'ctx'), partner(order[-1], number, over))  0.93 us
    ppermute x1, starting transfers between devices, paired(): halo = lax.ppermute(urgent, 'ctx', across)  0.81 us
    ppermute x1, starting transfers between devices, paired(): late = lax.ppermute(base, 'ctx', across)  0.8 us
  transfers between devices with their start and end apart: 12, of which 5 were waited for; matrix products, arithmetic and copies ran while one was open for 0% of the time, Pallas kernels for 35%

profile of v2, /device:TPU:0, one launch (start us, length us, event | category | flops | bytes accessed | tf_op | source)
XLA Modules:
  0.0 33.2 jit_solution(11947309550740928940)
XLA Ops:
  0.6 1.2 %first.1.refs_4_ = bf16[128,1024]{1,0:T(8,128)(2,1)S(1)} custom-call(bf16[128,2048]{1,0:T(8,128)(2,1)} %bitcast.9, bf16[128,2048]{1,0:T(8,128)(2,1)} %bitcast.11, bf16[128,2048]{1,0:T(8,128)(2,1)} %bitcast.13, bf16[128,2048]{1,0:T(8,128)(2,1)} %bitcast.15), custom_call_target="tpu_custom_call" | custom-call | tf_op jit(solution)/shard_map/first/pallas_call | solution.py:452
  1.8 0.0 copy-start
  1.8 0.8 %collective-permute-start.4 = (bf16[128,1024]{1,0:T(8,128)(2,1)S(1)}, bf16[128,1024]{1,0:T(8,128)(2,1)S(1)}, u32[]{:S(2)}, u32[]{:S(2)}) collective-permute-start(bf16[128,1024]{1,0:T(8,128)(2,1)S(1)} %first.1.refs_4_), channel_id=1, source_target_pairs={{1,2},{3,4},{5,6},{7,8},{9,10},{11,12},{13,14},{2,1},{4,3},{6,5},{... | collective-permute-start | bytes 786440 | tf_op jit(solution)/shard_map/ppermute | solution.py:521
  2.7 1.8 %prepare.1 = (bf16[128,2048]{1,0:T(8,128)(2,1)S(1)}, bf16[128,2048]{1,0:T(8,128)(2,1)S(1)}, bf16[128,2048]{1,0:T(8,128)(2,1)S(1)}, bf16[128,2048]{1,0:T(8,128)(2...) custom-call(bf16[128,2048]{1,0:T(8,128)(2,1)} %bitcast.10, ...), custom_call_target="tpu_custom_call" | custom-call | tf_op jit(solution)/shard_map/prepare/pallas_call | solution.py:452
  4.5 4.4 %collective-permute-start = (bf16[128,768]{1,0:T(8,128)(2,1)S(1)}, bf16[128,768]{1,0:T(8,128)(2,1)S(1)}, u32[]{:S(2)}, u32[]{:S(2)}) collective-permute-start(bf16[128,768]{1,0:T(8,128)(2,1)S(1)} %get-tuple-element.40.refs_0_), channel_id=1, source_target_pairs={{0,1},{1,0},{2,3},{3,2},{4,5},{5,4},{6,7},{7,6},{8,9},{9,8},{10,11... | collective-permute-start | bytes 589832 | tf_op jit(solution)/shard_map/ppermute | solution.py:530
  8.9 0.1 collective-permute-start.1
  8.9 0.4 %collective-permute-start.2 = (bf16[128,768]{1,0:T(8,128)(2,1)S(1)}, bf16[128,768]{1,0:T(8,128)(2,1)S(1)}, u32[]{:S(2)}, u32[]{:S(2)}) collective-permute-start(bf16[128,768]{1,0:T(8,128)(2,1)S(1)} %get-tuple-element.42.refs_2_), channel_id=1, source_target_pairs={{0,1},{1,0},{2,3},{3,2},{4,5},{5,4},{6,7},{7,6},{8,9},{9,8},{10,11... | collective-permute-start | bytes 589832 | tf_op jit(solution)/shard_map/ppermute | solution.py:530
  9.4 0.1 collective-permute-start.3
  9.4 0.5 %collective-permute-done.refs_4_ = bf16[128,768]{1,0:T(8,128)(2,1)S(1)} collective-permute-done((bf16[128,768]{1,0:T(8,128)(2,1)S(1)}, bf16[128,768]{1,0:T(8,128)(2,1)S(1)}, u32[]{:S(2)}, u32[]{:S(2)}) %collective-permute-start) | collective-permute-done | bytes 196640 | tf_op jit(solution)/shard_map/ppermute | solution.py:530
  9.9 0.0 copy-start.1
  9.9 0.8 %collective-permute-start.5 = (bf16[128,1024]{1,0:T(8,128)(2,1)S(1)}, bf16[128,1024]{1,0:T(8,128)(2,1)S(1)}, u32[]{:S(2)}, u32[]{:S(2)}) collective-permute-start(bf16[128,1024]{1,0:T(8,128)(2,1)S(1)} %get-tuple-element.44.base), channel_id=1, source_target_pairs={{1,2},{3,4},{5,6},{7,8},{9,10},{11,12},{13,14},{2,1},{4,3},{6,5},{... | collective-permute-start | bytes 786440 | tf_op jit(solution)/shard_map/ppermute | solution.py:529
  10.7 0.0 collective-permute-done.1.refs_5_
  10.7 0.0 collective-permute-done.2.refs_6_
  10.8 0.1 collective-permute-done.3.refs_7_
  10.9 0.0 copy-done
  10.9 1.0 %inside.1 = (f32[256,1024]{1,0:T(8,128)S(1)}, f32[256,1024]{1,0:T(8,128)S(1)}) custom-call(bf16[256,256]{1,0:T(8,128)(2,1)S(1)} %copy-done, bf16[128,1024]{1,0:T(8,128)(2,1)S(1)} %get-tuple-element.44.base, bf16[128,768]{1,0:T(8,128)(2,1)S(1)} %get-tuple-element.40.refs_0_, bf16[128,768]{1,0:T(8,128)(2,1)S(1)} %get-tuple-element.41.refs_1_, ...), custom_call_target="tpu_custom_call" | custom-call | tf_op jit(solution)/shard_map/inside/pallas_call | solution.py:452
  11.8 0.0 collective-permute-done.4.halo.refs_9_
  11.8 0.0 copy-done.1
  11.8 1.0 %lags.2 = (f32[2,128,128]{2,1,0:T(8,128)S(1)}, bf16[2,128,128]{2,1,0:T(8,128)(2,1)S(1)}, bf16[2,128,128]{2,1,0:T(8,128)(2,1)S(1)}, bf16[2,128,128]{2,1,0:T(8,128)(2,1)S(1)}) custom-call(bf16[256,256]{1,0:T(8,128)(2,1)S(1)} %copy-done, bf16[2,128,768]{2,1,0:T(8,128)(2,1)S(1)} %copy-done.1, bf16[128,1024]{1,0:T(8,128)(2,1)S(1)} %collective-permute-done.4.halo.refs_9_, ...), custom_call_target="tpu_custom_call" | custom-call | tf_op jit(solution)/shard_map/lags/pallas_call | solution.py:452
  12.8 5.2 %collective-permute-start.6 = (bf16[2,128,128]{2,1,0:T(8,128)(2,1)S(1)}, bf16[2,128,128]{2,1,0:T(8,128)(2,1)S(1)}, u32[]{:S(2)}, u32[]{:S(2)}) collective-permute-start(bf16[2,128,128]{2,1,0:T(8,128)(2,1)S(1)} %get-tuple-element.52), channel_id=1, source_target_pairs={{0,8},{1,9},{2,10},{3,11},{4,12},{5,13},{6,14},{7,15},{8,0},{9,1},... | collective-permute-start | bytes 196616 | tf_op jit(solution)/shard_map/ppermute | solution.py:575
  18.0 1.3 %collective-permute-start.7 = (bf16[2,128,128]{2,1,0:T(8,128)(2,1)S(1)}, bf16[2,128,128]{2,1,0:T(8,128)(2,1)S(1)}, u32[]{:S(2)}, u32[]{:S(2)}) collective-permute-start(bf16[2,128,128]{2,1,0:T(8,128)(2,1)S(1)} %get-tuple-element.53), channel_id=1, source_target_pairs={{0,12},{1,13},{2,14},{3,15},{4,8},{5,9},{6,10},{7,11},{8,4},{9,5},... | collective-permute-start | bytes 196616 | tf_op jit(solution)/shard_map/ppermute | solution.py:575
  19.4 0.2 collective-permute-start.8
  19.6 3.7 %inside_way.1 = (bf16[2,128,2048]{2,1,0:T(8,128)(2,1)S(1)}, bf16[256,512]{1,0:T(8,128)(2,1)S(1)}, bf16[128,768]{1,0:T(8,128)(2,1)S(1)}, bf16[128,768]{1,0:T(8,128)(2,1)S(1)}, bf16[128,2048]{1,0:T(8,128)(2,1)S(1)}) custom-call(bf16[128,2048]{1,0:T(8,128)(2,1)S(1)} %get-tuple-element.36.query.refs_0_, bf16[128,2048]{1,0:T(8,128)(2,1)S(1)} %get-tuple-element.37.key.refs_1_, ...), custom_call_target="tpu_custom_call" | custom-call | flops 3000000000 | tf_op jit(solution)/shard_map/inside_way/pallas_call | solution.py:452
  23.4 1.7 %across_first.1 = (bf16[128,2048]{1,0:T(8,128)(2,1)}, bf16[128,2048]{1,0:T(8,128)(2,1)}, bf16[128,2048]{1,0:T(8,128)(2,1)}, bf16[128,2048]{1,0:T(8,128)(2,1)}, bf16[2,128,2048]{2,1,0:T(8,128)(2,1)S(1)}) custom-call(bf16[128,2048]{1,0:T(8,128)(2,1)S(1)} %get-tuple-element.36.query.refs_0_, bf16[128,2048]{1,0:T(8,128)(2,1)S(1)} %get-tuple-element.37.key.refs_1_, ...), custom_call_target="tpu_custom_call" | custom-call | flops 3000000000 | tf_op jit(solution)/shard_map/across_first/pallas_call | solution.py:452
  25.0 0.2 collective-permute-done.6.refs_0_
  25.3 0.0 collective-permute-done.7.refs_1_
  25.3 0.3 collective-permute-done.8.refs_2_
  25.6 1.8 %collective-permute-start.11 = (bf16[1,128,128]{2,1,0:T(8,128)(2,1)S(1)}, bf16[1,128,128]{2,1,0:T(8,128)(2,1)S(1)}, u32[]{:S(2)}, u32[]{:S(2)}) collective-permute-start(bf16[1,128,128]{2,1,0:T(8,128)(2,1)S(1)} %get-tuple-element.66), channel_id=1, source_target_pairs={{0,18},{1,19},{2,16},{3,17},{4,22},{5,23},{6,20},{7,21},{8,26},{9,... | collective-permute-start | bytes 98312 | tf_op jit(solution)/shard_map/ppermute | solution.py:587
  27.3 1.3 %collective-permute-start.9 = (bf16[1,128,128]{2,1,0:T(8,128)(2,1)S(1)}, bf16[1,128,128]{2,1,0:T(8,128)(2,1)S(1)}, u32[]{:S(2)}, u32[]{:S(2)}) collective-permute-start(bf16[1,128,128]{2,1,0:T(8,128)(2,1)S(1)} %get-tuple-element.66), channel_id=1, source_target_pairs={{0,2},{1,3},{2,0},{3,1},{4,6},{5,7},{6,4},{7,5},{8,10},{9,11},{10,... | collective-permute-start | bytes 98312 | tf_op jit(solution)/shard_map/ppermute | solution.py:587
  28.6 0.5 %collective-permute-start.10 = (bf16[1,128,128]{2,1,0:T(8,128)(2,1)S(1)}, bf16[1,128,128]{2,1,0:T(8,128)(2,1)S(1)}, u32[]{:S(2)}, u32[]{:S(2)}) collective-permute-start(bf16[1,128,128]{2,1,0:T(8,128)(2,1)S(1)} %get-tuple-element.57.refs_10_.refs_0_), channel_id=1, source_target_pairs={{0,16},{1,17},{2,18},{3,19},{4,20},{5,21},{6,22},{7,23},{8,24},{9,... | collective-permute-start | bytes 98312 | tf_op jit(solution)/shard_map/ppermute | solution.py:587
  29.1 0.0 collective-permute-done.5.refs_9_
  29.1 2.4 %across_late.1 = (bf16[128,2048]{1,0:T(8,128)(2,1)}, bf16[128,2048]{1,0:T(8,128)(2,1)}, bf16[128,2048]{1,0:T(8,128)(2,1)}, bf16[128,2048]{1,0:T(8,128)(2,1)}, bf16[2,128,2048]{2,1,0:T(8,128)(2,1)S(1)}) custom-call(bf16[128,2048]{1,0:T(8,128)(2,1)S(1)} %get-tuple-element.36.query.refs_0, ...), custom_call_target="tpu_custom_call", output_to_operand_aliasing={{0}: (11, {}), {1}: (12, {}), {2}: (13, {}), {3}: (14, {}),... | custom-call | tf_op jit(solution)/shard_map/across_late/pallas_call | solution.py:452
  31.6 0.0 collective-permute-done.11.refs_3_
  31.6 0.0 collective-permute-done.9.refs_1_
  31.6 0.9 %collective-permute-done.10.refs_2_ = bf16[1,128,128]{2,1,0:T(8,128)(2,1)S(1)} collective-permute-done((bf16[1,128,128]{2,1,0:T(8,128)(2,1)S(1)}, bf16[1,128,128]{2,1,0:T(8,128)(2,1)S(1)}, u32[]{:S(2)}, u32[]{:S(2)}) %collective-permute-start.10) | collective-permute-done | bytes 32800 | tf_op jit(solution)/shard_map/ppermute | solution.py:587
  32.5 0.7 %total.1 = f32[128,128]{1,0:T(8,128)} custom-call(bf16[1,128,128]{2,1,0:T(8,128)(2,1)S(1)} %get-tuple-element.57.refs_10_.refs_0_, bf16[1,128,128]{2,1,0:T(8,128)(2,1)S(1)} %collective-permute-done.9.refs_1_, bf16[1,128,128]{2,1,0:T(8,128)(2,1)S(1)} %collective-permute-done.10.refs_2_, bf16[1,128,128]{2,1,0:T(8,128)(2,1)S(1)} %collective-permute-done.11.refs_3_, ...), custom_call_target="tpu_custom_call" | custom-call | tf_op jit(solution)/shard_map/total/pallas_call | solution.py:452
  (1 shorter events, 0.0 us)
Async XLA Ops:
  1.8 9.0 %copy-start = (bf16[256,256]{1,0:T(8,128)(2,1)S(1)}, bf16[256,256]{1,0:T(8,128)(2,1)}, u32[]{:S(2)}) copy-start(bf16[256,256]{1,0:T(8,128)(2,1)} %constant.10.clone.one.refs_4_) | copy-start | bytes 393220
  1.8 10.0 %collective-permute-start.4 = (bf16[128,1024]{1,0:T(8,128)(2,1)S(1)}, bf16[128,1024]{1,0:T(8,128)(2,1)S(1)}, u32[]{:S(2)}, u32[]{:S(2)}) collective-permute-start(bf16[128,1024]{1,0:T(8,128)(2,1)S(1)} %first.1.refs_4_), channel_id=1, source_target_pairs={{1,2},{3,4},{5,6},{7,8},{9,10},{11,12},{13,14},{2,1},{4,3},{6,5},{... | collective-permute-start | bytes 786440 | tf_op jit(solution)/shard_map/ppermute | solution.py:521
  4.5 5.4 %collective-permute-start = (bf16[128,768]{1,0:T(8,128)(2,1)S(1)}, bf16[128,768]{1,0:T(8,128)(2,1)S(1)}, u32[]{:S(2)}, u32[]{:S(2)}) collective-permute-start(bf16[128,768]{1,0:T(8,128)(2,1)S(1)} %get-tuple-element.40.refs_0_), channel_id=1, source_target_pairs={{0,1},{1,0},{2,3},{3,2},{4,5},{5,4},{6,7},{7,6},{8,9},{9,8},{10,11... | collective-permute-start | bytes 589832 | tf_op jit(solution)/shard_map/ppermute | solution.py:530
  8.9 1.9 %collective-permute-start.1 = (bf16[128,768]{1,0:T(8,128)(2,1)S(1)}, bf16[128,768]{1,0:T(8,128)(2,1)S(1)}, u32[]{:S(2)}, u32[]{:S(2)}) collective-permute-start(bf16[128,768]{1,0:T(8,128)(2,1)S(1)} %get-tuple-element.41.refs_1_), channel_id=1, source_target_pairs={{0,1},{1,0},{2,3},{3,2},{4,5},{5,4},{6,7},{7,6},{8,9},{9,8},{10,11... | collective-permute-start | bytes 589832 | tf_op jit(solution)/shard_map/ppermute | solution.py:530
  8.9 1.8 %collective-permute-start.2 = (bf16[128,768]{1,0:T(8,128)(2,1)S(1)}, bf16[128,768]{1,0:T(8,128)(2,1)S(1)}, u32[]{:S(2)}, u32[]{:S(2)}) collective-permute-start(bf16[128,768]{1,0:T(8,128)(2,1)S(1)} %get-tuple-element.42.refs_2_), channel_id=1, source_target_pairs={{0,1},{1,0},{2,3},{3,2},{4,5},{5,4},{6,7},{7,6},{8,9},{9,8},{10,11... | collective-permute-start | bytes 589832 | tf_op jit(solution)/shard_map/ppermute | solution.py:530
  9.4 1.5 %collective-permute-start.3 = (bf16[128,768]{1,0:T(8,128)(2,1)S(1)}, bf16[128,768]{1,0:T(8,128)(2,1)S(1)}, u32[]{:S(2)}, u32[]{:S(2)}) collective-permute-start(bf16[128,768]{1,0:T(8,128)(2,1)S(1)} %get-tuple-element.43.refs_3_), channel_id=1, source_target_pairs={{0,1},{1,0},{2,3},{3,2},{4,5},{5,4},{6,7},{7,6},{8,9},{9,8},{10,11... | collective-permute-start | bytes 589832 | tf_op jit(solution)/shard_map/ppermute | solution.py:530
  9.9 1.9 %copy-start.1 = (bf16[2,128,768]{2,1,0:T(8,128)(2,1)S(1)}, bf16[2,128,768]{2,1,0:T(8,128)(2,1)}, u32[]{:S(2)}) copy-start(bf16[2,128,768]{2,1,0:T(8,128)(2,1)} %constant.11.clone.lags) | copy-start | bytes 1179652
  9.9 19.2 %collective-permute-start.5 = (bf16[128,1024]{1,0:T(8,128)(2,1)S(1)}, bf16[128,1024]{1,0:T(8,128)(2,1)S(1)}, u32[]{:S(2)}, u32[]{:S(2)}) collective-permute-start(bf16[128,1024]{1,0:T(8,128)(2,1)S(1)} %get-tuple-element.44.base), channel_id=1, source_target_pairs={{1,2},{3,4},{5,6},{7,8},{9,10},{11,12},{13,14},{2,1},{4,3},{6,5},{... | collective-permute-start | bytes 786440 | tf_op jit(solution)/shard_map/ppermute | solution.py:529
  12.8 12.4 %collective-permute-start.6 = (bf16[2,128,128]{2,1,0:T(8,128)(2,1)S(1)}, bf16[2,128,128]{2,1,0:T(8,128)(2,1)S(1)}, u32[]{:S(2)}, u32[]{:S(2)}) collective-permute-start(bf16[2,128,128]{2,1,0:T(8,128)(2,1)S(1)} %get-tuple-element.52), channel_id=1, source_target_pairs={{0,8},{1,9},{2,10},{3,11},{4,12},{5,13},{6,14},{7,15},{8,0},{9,1},... | collective-permute-start | bytes 196616 | tf_op jit(solution)/shard_map/ppermute | solution.py:575
  18.0 7.2 %collective-permute-start.7 = (bf16[2,128,128]{2,1,0:T(8,128)(2,1)S(1)}, bf16[2,128,128]{2,1,0:T(8,128)(2,1)S(1)}, u32[]{:S(2)}, u32[]{:S(2)}) collective-permute-start(bf16[2,128,128]{2,1,0:T(8,128)(2,1)S(1)} %get-tuple-element.53), channel_id=1, source_target_pairs={{0,12},{1,13},{2,14},{3,15},{4,8},{5,9},{6,10},{7,11},{8,4},{9,5},... | collective-permute-start | bytes 196616 | tf_op jit(solution)/shard_map/ppermute | solution.py:575
  19.4 6.2 %collective-permute-start.8 = (bf16[2,128,128]{2,1,0:T(8,128)(2,1)S(1)}, bf16[2,128,128]{2,1,0:T(8,128)(2,1)S(1)}, u32[]{:S(2)}, u32[]{:S(2)}) collective-permute-start(bf16[2,128,128]{2,1,0:T(8,128)(2,1)S(1)} %get-tuple-element.54), channel_id=1, source_target_pairs={{0,4},{1,5},{2,6},{3,7},{4,0},{5,1},{6,2},{7,3},{8,12},{9,13},{10,... | collective-permute-start | bytes 196616 | tf_op jit(solution)/shard_map/ppermute | solution.py:575
  25.6 6.0 %collective-permute-start.11 = (bf16[1,128,128]{2,1,0:T(8,128)(2,1)S(1)}, bf16[1,128,128]{2,1,0:T(8,128)(2,1)S(1)}, u32[]{:S(2)}, u32[]{:S(2)}) collective-permute-start(bf16[1,128,128]{2,1,0:T(8,128)(2,1)S(1)} %get-tuple-element.66), channel_id=1, source_target_pairs={{0,18},{1,19},{2,16},{3,17},{4,22},{5,23},{6,20},{7,21},{8,26},{9,... | collective-permute-start | bytes 98312 | tf_op jit(solution)/shard_map/ppermute | solution.py:587
  27.3 4.2 %collective-permute-start.9 = (bf16[1,128,128]{2,1,0:T(8,128)(2,1)S(1)}, bf16[1,128,128]{2,1,0:T(8,128)(2,1)S(1)}, u32[]{:S(2)}, u32[]{:S(2)}) collective-permute-start(bf16[1,128,128]{2,1,0:T(8,128)(2,1)S(1)} %get-tuple-element.66), channel_id=1, source_target_pairs={{0,2},{1,3},{2,0},{3,1},{4,6},{5,7},{6,4},{7,5},{8,10},{9,11},{10,... | collective-permute-start | bytes 98312 | tf_op jit(solution)/shard_map/ppermute | solution.py:587
  28.6 3.9 %collective-permute-start.10 = (bf16[1,128,128]{2,1,0:T(8,128)(2,1)S(1)}, bf16[1,128,128]{2,1,0:T(8,128)(2,1)S(1)}, u32[]{:S(2)}, u32[]{:S(2)}) collective-permute-start(bf16[1,128,128]{2,1,0:T(8,128)(2,1)S(1)} %get-tuple-element.57.refs_10_.refs_0_), channel_id=1, source_target_pairs={{0,16},{1,17},{2,18},{3,19},{4,20},{5,21},{6,22},{7,23},{8,24},{9,... | collective-permute-start | bytes 98312 | tf_op jit(solution)/shard_map/ppermute | solution.py:587

commit v3 on v2

--- a/solution.py
+++ b/solution.py
@@ -34,8 +34,6 @@
     real, imag = np.cos(phase), np.sin(phase)
     one = np.concatenate([real, imag], axis=0)
     pair = np.concatenate([one, np.concatenate([-imag, real], axis=0)], axis=1)
-    upper = np.concatenate([-imag.T, real.T], axis=1) / size
-    lower = np.concatenate([real.T, imag.T], axis=1) / size
     lag = (size - np.arange(taps))[:, None] * angle[None, :]
     lags = np.concatenate([np.cos(lag), np.sin(lag)], axis=1) / size
     turned = np.concatenate([imag.T, -real.T], axis=1)[:taps] / size
@@ -51,8 +49,6 @@
         forward(one[:, :taps]),
         forward(one),
         forward(pair),
-        inverse(upper),
-        inverse(lower),
         np.stack([inverse(lags), inverse(turned)]),
     )
 
@@ -87,13 +83,14 @@
     return (left.astype(f32) * right.astype(f32)).astype(bf16)
 
 
-def forward_strip(pair, upper, before, kv, weights, query, grad):
-    mixed = back(upper, *times(spectrum(pair, before, kv), weights))
+def forward_strip(pair, turned, before, kv, weights, query, grad):
+    mixed = -back(turned, *times(spectrum(pair, before, kv), weights))
     return (query.astype(f32) * mixed).astype(bf16), (grad.astype(f32) * mixed).astype(bf16)
 
 
-def backward_strip(pair, lower, gate, beyond, weights, key, value):
-    flowing = back(lower, *times_conjugate(spectrum(pair, gate, beyond), weights))
+def backward_strip(pair, turned, gate, beyond, weights, key, value):
+    real, imag = times_conjugate(spectrum(pair, gate, beyond), weights)
+    flowing = back(turned, imag, -real)
     return (flowing * value.astype(f32)).astype(bf16), (flowing * key.astype(f32)).astype(bf16)
 
 
@@ -191,16 +188,16 @@
 
 
 def prepare_kernel(share, *refs):
-    sources, held, base, sends, sems = refs[:4], refs[5:9], refs[9], refs[10:-1], refs[-1]
-    query, grad, key, value = held
+    sources, held, base, sends = refs[:4], refs[5:9], refs[9], refs[10:]
+    query, grad, key, value = sources
     half, width = base.shape[1], sends[0].shape[1]
-    rows, groups = start_loads(sources, held, sems)
 
     def run(parity):
         pairs = (key, value), (query, grad)
         first, second = pairs if parity == 0 else pairs[::-1]
-        for part, group in zip(rows, groups):
-            wait(group)
+        for part in rows_of(base, base.shape[0] // load_rows):
+            for source, place in zip(sources, held):
+                place[part] = source[part]
             for offset in range(0, half, lanes):
                 start = 2 * (offset // share) * share + offset % share
                 own = slice(start + parity * share, start + parity * share + lanes)
@@ -299,19 +296,23 @@
             held[which, :, cols] = result[:, number * share : (number + 1) * share]
 
 
-def inside_way_kernel(share, query, key, value, grad, one, *refs):
-    fetched, came, refs = refs[:4], refs[4 : 4 + pieces_inside], refs[5 + pieces_inside :]
-    held, *placed, sems = refs
-    pair, upper, lower, taps = placed
+def make_pair(one, pair):
+    size = one.shape[0] // 2
+    for part in range(2):
+        real = one[:size, part * size : (part + 1) * size]
+        imag = one[size:, part * size : (part + 1) * size]
+        start = 2 * part * size
+        pair[:size, start : start + size] = real
+        pair[size:, start : start + size] = imag
+        pair[:size, start + size : start + 2 * size] = -imag
+        pair[size:, start + size : start + 2 * size] = real
+
+
+def inside_way_kernel(share, query, key, value, grad, one, lags, taps_in, *refs):
+    came, (held, pair, taps) = refs[:pieces_inside], refs[1 + pieces_inside :]
     half = taps.shape[1] // 2
-    fetches = [
-        pltpu.make_async_copy(source.at[rows], place.at[rows], sems.at[number, part])
-        for number, (source, place) in enumerate(zip(fetched, placed))
-        for part, rows in enumerate(rows_of(place, sems.shape[1]))
-    ]
-    for fetch in fetches:
-        fetch.start()
-    wait(fetches)
+    taps[...] = taps_in[...]
+    make_pair(one, pair)
 
     def run(parity):
         for number in range(half // tile):
@@ -324,11 +325,11 @@
                 within = gather(key, columns), gather(value, columns)
                 if parity == 0:
                     results = backward_strip(
-                        pair[...], lower[...], product(*around), halo, weights, *within
+                        pair[...], lags[1], product(*around), halo, weights, *within
                     )
                 else:
                     results = forward_strip(
-                        pair[...], upper[...], halo, product(*within), weights, *around
+                        pair[...], lags[1], halo, product(*within), weights, *around
                     )
                 spread(held, results, columns, share)
 
@@ -337,7 +338,7 @@
 
 
 def across_way(share, late, parity, held, after, *refs):
-    query, key, value, grad, one, pair, upper, lower, taps, halo = refs
+    query, key, value, grad, one, lags, pair, taps, halo = refs
 
     def body(number, packed):
         columns = blocks(1 - parity if late else parity, number, share)
@@ -346,11 +347,11 @@
         within = gather(key, columns), gather(value, columns)
         if parity == 0:
             results = forward_strip(
-                pair[...], upper[...], halo[:, packed], product(*within), weights, *around
+                pair[...], lags[1], halo[:, packed], product(*within), weights, *around
             )
         else:
             results = backward_strip(
-                pair[...], lower[...], product(*around), halo[:, packed], weights, *within
+                pair[...], lags[1], product(*around), halo[:, packed], weights, *within
             )
         spread(held, results, columns, share)
         after(number)
@@ -359,7 +360,7 @@
 
 
 def across_first_kernel(share, *refs):
-    inputs, before, refs = refs[:10], refs[10], refs[12:]
+    inputs, before, refs = refs[:9], refs[9], refs[11:]
     outs, held, sems = refs[:4], refs[4], refs[5]
 
     def run(parity):
@@ -379,7 +380,7 @@
 
 
 def across_late_kernel(share, *refs):
-    inputs, refs = refs[:10], refs[16:]
+    inputs, refs = refs[:9], refs[15:]
     outs, held, sems = refs[:4], refs[4], refs[5]
 
     def run(parity):
@@ -424,17 +425,17 @@
 
 
 def plain_filter_kernel(
-    first, pair, upper, lower, before, kv, gate, beyond, taps, query, key, value, grad,
+    first, pair, lags, before, kv, gate, beyond, taps, query, key, value, grad,
     output, grad_query, grad_key, grad_value,
 ):
     for cols in tiles(kv):
         weights = spectrum(first[...], taps[:, cols])
         output[:, cols], grad_query[:, cols] = forward_strip(
-            pair[...], upper[...], before[:, cols], kv[:, cols], weights,
+            pair[...], lags[1], before[:, cols], kv[:, cols], weights,
             query[:, cols], grad[:, cols],
         )
         grad_key[:, cols], grad_value[:, cols] = backward_strip(
-            pair[...], lower[...], gate[:, cols], beyond[:, cols], weights,
+            pair[...], lags[1], gate[:, cols], beyond[:, cols], weights,
             key[:, cols], value[:, cols],
         )
 
@@ -504,7 +505,7 @@
     ctx = lax.axis_size("ctx")
     share = channels // ctx
     half = channels // 2
-    _, one, pair, upper, lower, lags = transforms(length, taps)
+    _, one, _, lags = transforms(length, taps)
     block, strip = shape((length, channels), bf16), shape((length, half), bf16)
     spectra = shape((2 * length, half), f32)
     sources = query, grad, key, value
@@ -523,8 +524,6 @@
     query, grad, key, value, base, *sends = call(
         functools.partial(prepare_kernel, share), "prepare", (*sources, urgent),
         [block] * 4 + [strip] + [piece] * pieces_inside,
-        far_ins=range(4),
-        scratch=[pltpu.SemaphoreType.DMA((4, length // load_rows))],
     )
     late = lax.ppermute(base, "ctx", across)
     came = [lax.ppermute(send, "ctx", inside) for send in sends]
@@ -548,19 +547,16 @@
         split(order[0], len(order) == 1),
         scratch=[pltpu.VMEM((ctx // 2, taps, share), f32)],
     )
-    held = query, key, value, grad, one
-    fetched = pair, upper, lower, filter_taps
+    held = query, key, value, grad, one, lags
     wide = shape((2, length, channels), bf16)
-    inner, *fetched = call(
+    inner, *made = call(
         functools.partial(inside_way_kernel, share), "inside_way",
-        (*held, *fetched, *came, keep),
-        [wide] + [shape(array.shape, bf16) for array in fetched],
-        far_ins=range(5, 9),
-        scratch=[pltpu.SemaphoreType.DMA((len(fetched), 4))],
+        (*held, filter_taps, *came, keep),
+        [wide, shape((2 * length, 4 * length), bf16), block],
         limit=large_bytes,
         flops=3 * 10**9,
     )
-    held = *held, *fetched
+    held = *held, *made
     *results, outer = call(
         functools.partial(across_first_kernel, share), "across_first",
         (*held, halo, inner, keep),
@@ -594,9 +590,9 @@
         functools.partial(across_late_kernel, share), "across_late",
         (*held, late, keep, *results, outer),
         [block] * 4 + [wide],
-        far_ins=range(11, 15),
+        far_ins=range(10, 14),
         far_outs=range(4),
-        input_output_aliases={11 + at: at for at in range(5)},
+        input_output_aliases={10 + at: at for at in range(5)},
         scratch=[pltpu.SemaphoreType.DMA((half // tile, 2, 2))],
         limit=large_bytes,
     )
@@ -616,7 +612,7 @@
     taps = filter_taps.shape[0]
     ctx = lax.axis_size("ctx")
     share = channels // ctx
-    first, one, pair, upper, lower, lags = transforms(length, taps)
+    first, one, pair, lags = transforms(length, taps)
     block = shape((length, channels), bf16)
     query, grad, key, value, kv, gate = call(
         plain_load_kernel, "load", (query, grad, key, value), [block] * 6,
@@ -633,7 +629,7 @@
     total = total * (1.0 / math.sqrt(length * ctx * lax.axis_size("dp")))
     results = call(
         plain_filter_kernel, "filters",
-        (first, pair, upper, lower, before, kv, gate, beyond, filter_taps)
+        (first, pair, lags, before, kv, gate, beyond, filter_taps)
         + (query, key, value, grad),
         [block] * 4,
     )

time: 33.4 us -> 32 us (0.958)
  Pallas kernels: 13.5 us -> 10.8 us
  waiting for transfers between devices: 2.01 us -> 3.18 us
    pallas_call x9, Pallas kernels: 13.5 us -> 10.8 us  [call(): pl.pallas_call(kernel, in_specs=[pl.BlockSpec(memory_space=space(at)) for...]
    ppermute x3, waiting for transfers between devices: 0.48 us -> 1.66 us  [paired(): lax.ppermute(sends[number - 1], ('dp', 'ctx'), partner(level, number))]
  transfers between devices with their start and end apart: 12 -> 12, of which waited for: 5 -> 6; matrix products, arithmetic and copies ran while one was open for 0% -> 0% of each run, Pallas kernels for 35% -> 28%
where the time goes in v3:
time: 32 us; the launch traced here: 31.8 us
  starting transfers between devices  16.9 us (53%)
  Pallas kernels  10.8 us (34%)
  waiting for transfers between devices  3.18 us (10%)
  between operations  0.84 us (3%)
    pallas_call x9, Pallas kernels, call(): pl.pallas_call(kernel, in_specs=[pl.BlockSpec(memory_space=space(at)) for...  10.8 us
    ppermute x3, starting transfers between devices, paired(): lax.ppermute(sends[number - 1], ('dp', 'ctx'), partner(level, number))  6.78 us
    ppermute x4, starting transfers between devices, paired(): came = [lax.ppermute(send, 'ctx', inside) for send in sends]  4.96 us
    ppermute x3, starting transfers between devices, paired(): lax.ppermute(send, ('dp', 'ctx'), partner(order[-1], number, over))  3.55 us
    ppermute x3, waiting for transfers between devices, paired(): lax.ppermute(sends[number - 1], ('dp', 'ctx'), partner(level, number))  1.66 us
    ppermute x3, waiting for transfers between devices, paired(): lax.ppermute(send, ('dp', 'ctx'), partner(order[-1], number, over))  0.93 us
    ppermute x1, starting transfers between devices, paired(): halo = lax.ppermute(urgent, 'ctx', across)  0.81 us
    ppermute x1, starting transfers between devices, paired(): late = lax.ppermute(base, 'ctx', across)  0.8 us
  transfers between devices with their start and end apart: 12, of which 6 were waited for; matrix products, arithmetic and copies ran while one was open for 0% of the time, Pallas kernels for 28%

profile of v3, /device:TPU:0, one launch (start us, length us, event | category | flops | bytes accessed | tf_op | source)
XLA Modules:
  0.0 31.8 jit_solution(16494477440057027441)
XLA Ops:
  0.6 0.0 copy-start
  0.6 0.0 copy-start.1
  0.7 0.0 copy-start.2
  0.7 0.0 copy-start.3
  0.7 1.3 %first.1.refs_4_ = bf16[128,1024]{1,0:T(8,128)(2,1)S(1)} custom-call(bf16[128,2048]{1,0:T(8,128)(2,1)} %bitcast.8, bf16[128,2048]{1,0:T(8,128)(2,1)} %bitcast.10, bf16[128,2048]{1,0:T(8,128)(2,1)} %bitcast.12, bf16[128,2048]{1,0:T(8,128)(2,1)} %bitcast.14), custom_call_target="tpu_custom_call" | custom-call | tf_op jit(solution)/shard_map/first/pallas_call | solution.py:453
  2.0 0.0 copy-start.5
  2.0 0.8 %collective-permute-start.4 = (bf16[128,1024]{1,0:T(8,128)(2,1)S(1)}, bf16[128,1024]{1,0:T(8,128)(2,1)S(1)}, u32[]{:S(2)}, u32[]{:S(2)}) collective-permute-start(bf16[128,1024]{1,0:T(8,128)(2,1)S(1)} %first.1.refs_4_), channel_id=1, source_target_pairs={{1,2},{3,4},{5,6},{7,8},{9,10},{11,12},{13,14},{2,1},{4,3},{6,5},{... | collective-permute-start | bytes 786440 | tf_op jit(solution)/shard_map/ppermute | solution.py:522
  2.8 0.0 copy-done
  2.8 0.0 copy-done.1
  2.8 0.0 copy-done.2
  2.9 0.0 copy-done.3
  2.9 0.4 %prepare.1 = (bf16[128,2048]{1,0:T(8,128)(2,1)S(1)}, bf16[128,2048]{1,0:T(8,128)(2,1)S(1)}, bf16[128,2048]{1,0:T(8,128)(2,1)S(1)}, bf16[128,2048]{1,0:T(8,128)(2...) custom-call(bf16[128,2048]{1,0:T(8,128)(2,1)S(1)} %bitcast.9, ...), custom_call_target="tpu_custom_call" | custom-call | tf_op jit(solution)/shard_map/prepare/pallas_call | solution.py:453
  3.3 4.4 %collective-permute-start = (bf16[128,768]{1,0:T(8,128)(2,1)S(1)}, bf16[128,768]{1,0:T(8,128)(2,1)S(1)}, u32[]{:S(2)}, u32[]{:S(2)}) collective-permute-start(bf16[128,768]{1,0:T(8,128)(2,1)S(1)} %get-tuple-element.38.refs_0_), channel_id=1, source_target_pairs={{0,1},{1,0},{2,3},{3,2},{4,5},{5,4},{6,7},{7,6},{8,9},{9,8},{10,11... | collective-permute-start | bytes 589832 | tf_op jit(solution)/shard_map/ppermute | solution.py:529
  7.6 0.1 collective-permute-start.1
  7.7 0.4 %collective-permute-start.2 = (bf16[128,768]{1,0:T(8,128)(2,1)S(1)}, bf16[128,768]{1,0:T(8,128)(2,1)S(1)}, u32[]{:S(2)}, u32[]{:S(2)}) collective-permute-start(bf16[128,768]{1,0:T(8,128)(2,1)S(1)} %get-tuple-element.40.refs_2_), channel_id=1, source_target_pairs={{0,1},{1,0},{2,3},{3,2},{4,5},{5,4},{6,7},{7,6},{8,9},{9,8},{10,11... | collective-permute-start | bytes 589832 | tf_op jit(solution)/shard_map/ppermute | solution.py:529
  8.1 0.1 collective-permute-start.3
  8.2 0.5 %collective-permute-done.refs_4_.refs_0_ = bf16[128,768]{1,0:T(8,128)(2,1)S(1)} collective-permute-done((bf16[128,768]{1,0:T(8,128)(2,1)S(1)}, bf16[128,768]{1,0:T(8,128)(2,1)S(1)}, u32[]{:S(2)}, u32[]{:S(2)}) %collective-permute-start) | collective-permute-done | bytes 196640 | tf_op jit(solution)/shard_map/ppermute | solution.py:529
  8.7 0.0 copy-start.4
  8.7 0.8 %collective-permute-start.5 = (bf16[128,1024]{1,0:T(8,128)(2,1)S(1)}, bf16[128,1024]{1,0:T(8,128)(2,1)S(1)}, u32[]{:S(2)}, u32[]{:S(2)}) collective-permute-start(bf16[128,1024]{1,0:T(8,128)(2,1)S(1)} %get-tuple-element.42.base), channel_id=1, source_target_pairs={{1,2},{3,4},{5,6},{7,8},{9,10},{11,12},{13,14},{2,1},{4,3},{6,5},{... | collective-permute-start | bytes 786440 | tf_op jit(solution)/shard_map/ppermute | solution.py:528
  9.5 0.0 collective-permute-done.1.refs_5_.refs_1_
  9.5 0.0 collective-permute-done.2.refs_6_.refs_2_
  9.5 0.1 collective-permute-done.3.refs_7_.refs_3_
  9.6 0.0 copy-done.5
  9.6 1.0 %inside.1 = (f32[256,1024]{1,0:T(8,128)S(1)}, f32[256,1024]{1,0:T(8,128)S(1)}) custom-call(bf16[256,256]{1,0:T(8,128)(2,1)S(1)} %copy-done.5, bf16[128,1024]{1,0:T(8,128)(2,1)S(1)} %get-tuple-element.42.base, bf16[128,768]{1,0:T(8,128)(2,1)S(1)} %get-tuple-element.38.refs_0_, bf16[128,768]{1,0:T(8,128)(2,1)S(1)} %get-tuple-element.39.refs_1_, ...), custom_call_target="tpu_custom_call" | custom-call | tf_op jit(solution)/shard_map/inside/pallas_call | solution.py:453
  10.6 0.0 collective-permute-done.4.halo.refs_8_
  10.6 0.0 copy-done.4
  10.6 0.0 copy-start.6
  10.6 1.0 %lags.3 = (f32[2,128,128]{2,1,0:T(8,128)S(1)}, bf16[2,128,128]{2,1,0:T(8,128)(2,1)S(1)}, bf16[2,128,128]{2,1,0:T(8,128)(2,1)S(1)}, bf16[2,128,128]{2,1,0:T(8,128)(2,1)S(1)}) custom-call(bf16[256,256]{1,0:T(8,128)(2,1)S(1)} %copy-done.5, bf16[2,128,768]{2,1,0:T(8,128)(2,1)S(1)} %copy-done.4, bf16[128,1024]{1,0:T(8,128)(2,1)S(1)} %collective-permute-done.4.halo.refs_8_, ...), custom_call_target="tpu_custom_call" | custom-call | tf_op jit(solution)/shard_map/lags/pallas_call | solution.py:453
  11.6 5.2 %collective-permute-start.6 = (bf16[2,128,128]{2,1,0:T(8,128)(2,1)S(1)}, bf16[2,128,128]{2,1,0:T(8,128)(2,1)S(1)}, u32[]{:S(2)}, u32[]{:S(2)}) collective-permute-start(bf16[2,128,128]{2,1,0:T(8,128)(2,1)S(1)} %get-tuple-element.48), channel_id=1, source_target_pairs={{0,8},{1,9},{2,10},{3,11},{4,12},{5,13},{6,14},{7,15},{8,0},{9,1},... | collective-permute-start | bytes 196616 | tf_op jit(solution)/shard_map/ppermute | solution.py:571
  16.8 1.3 %collective-permute-start.7 = (bf16[2,128,128]{2,1,0:T(8,128)(2,1)S(1)}, bf16[2,128,128]{2,1,0:T(8,128)(2,1)S(1)}, u32[]{:S(2)}, u32[]{:S(2)}) collective-permute-start(bf16[2,128,128]{2,1,0:T(8,128)(2,1)S(1)} %get-tuple-element.49), channel_id=1, source_target_pairs={{0,12},{1,13},{2,14},{3,15},{4,8},{5,9},{6,10},{7,11},{8,4},{9,5},... | collective-permute-start | bytes 196616 | tf_op jit(solution)/shard_map/ppermute | solution.py:571
  18.2 0.2 collective-permute-start.8
  18.4 0.0 copy-done.6
  18.4 2.4 %inside_way.1 = (bf16[2,128,2048]{2,1,0:T(8,128)(2,1)S(1)}, bf16[256,512]{1,0:T(8,128)(2,1)S(1)}, bf16[128,2048]{1,0:T(8,128)(2,1)S(1)}) custom-call(bf16[128,2048]{1,0:T(8,128)(2,1)S(1)} %get-tuple-element.34.query.refs_0_, bf16[128,2048]{1,0:T(8,128)(2,1)S(1)} %get-tuple-element.35.key.refs_1_, bf16[128,2048]{1,0:T(8,128)(2,1)S(1)} %get-tuple-element.36.value.refs_2_, ...), custom_call_target="tpu_custom_call" | custom-call | flops 3000000000 | tf_op jit(solution)/shard_map/inside_way/pallas_call | solution.py:453
  20.8 1.7 %across_first.1 = (bf16[128,2048]{1,0:T(8,128)(2,1)}, bf16[128,2048]{1,0:T(8,128)(2,1)}, bf16[128,2048]{1,0:T(8,128)(2,1)}, bf16[128,2048]{1,0:T(8,128)(2,1)}, bf16[2,128,2048]{2,1,0:T(8,128)(2,1)S(1)}) custom-call(bf16[128,2048]{1,0:T(8,128)(2,1)S(1)} %get-tuple-element.34.query.refs_0_, bf16[128,2048]{1,0:T(8,128)(2,1)S(1)} %get-tuple-element.35.key.refs_1_, ...), custom_call_target="tpu_custom_call" | custom-call | flops 3000000000 | tf_op jit(solution)/shard_map/across_first/pallas_call | solution.py:453
  22.5 1.0 %collective-permute-done.6.refs_0_ = bf16[2,128,128]{2,1,0:T(8,128)(2,1)S(1)} collective-permute-done((bf16[2,128,128]{2,1,0:T(8,128)(2,1)S(1)}, bf16[2,128,128]{2,1,0:T(8,128)(2,1)S(1)}, u32[]{:S(2)}, u32[]{:S(2)}) %collective-permute-start.6) | collective-permute-done | bytes 65568 | tf_op jit(solution)/shard_map/ppermute | solution.py:571
  23.5 0.0 collective-permute-done.7.refs_1_
  23.5 0.6 %collective-permute-done.8.refs_2_ = bf16[2,128,128]{2,1,0:T(8,128)(2,1)S(1)} collective-permute-done((bf16[2,128,128]{2,1,0:T(8,128)(2,1)S(1)}, bf16[2,128,128]{2,1,0:T(8,128)(2,1)S(1)}, u32[]{:S(2)}, u32[]{:S(2)}) %collective-permute-start.8) | collective-permute-done | bytes 65568 | tf_op jit(solution)/shard_map/ppermute | solution.py:571
  24.2 2.4 %collective-permute-start.11 = (bf16[1,128,128]{2,1,0:T(8,128)(2,1)S(1)}, bf16[1,128,128]{2,1,0:T(8,128)(2,1)S(1)}, u32[]{:S(2)}, u32[]{:S(2)}) collective-permute-start(bf16[1,128,128]{2,1,0:T(8,128)(2,1)S(1)} %get-tuple-element.62), channel_id=1, source_target_pairs={{0,18},{1,19},{2,16},{3,17},{4,22},{5,23},{6,20},{7,21},{8,26},{9,... | collective-permute-start | bytes 98312 | tf_op jit(solution)/shard_map/ppermute | solution.py:583
  26.6 0.6 %collective-permute-start.9 = (bf16[1,128,128]{2,1,0:T(8,128)(2,1)S(1)}, bf16[1,128,128]{2,1,0:T(8,128)(2,1)S(1)}, u32[]{:S(2)}, u32[]{:S(2)}) collective-permute-start(bf16[1,128,128]{2,1,0:T(8,128)(2,1)S(1)} %get-tuple-element.62), channel_id=1, source_target_pairs={{0,2},{1,3},{2,0},{3,1},{4,6},{5,7},{6,4},{7,5},{8,10},{9,11},{10,... | collective-permute-start | bytes 98312 | tf_op jit(solution)/shard_map/ppermute | solution.py:583
  27.2 0.5 %collective-permute-start.10 = (bf16[1,128,128]{2,1,0:T(8,128)(2,1)S(1)}, bf16[1,128,128]{2,1,0:T(8,128)(2,1)S(1)}, u32[]{:S(2)}, u32[]{:S(2)}) collective-permute-start(bf16[1,128,128]{2,1,0:T(8,128)(2,1)S(1)} %get-tuple-element.53.refs_9_.refs_0_), channel_id=1, source_target_pairs={{0,16},{1,17},{2,18},{3,19},{4,20},{5,21},{6,22},{7,23},{8,24},{9,... | collective-permute-start | bytes 98312 | tf_op jit(solution)/shard_map/ppermute | solution.py:583
  27.8 0.0 collective-permute-done.5.refs_8_
  27.8 2.4 %across_late.1 = (bf16[128,2048]{1,0:T(8,128)(2,1)}, bf16[128,2048]{1,0:T(8,128)(2,1)}, bf16[128,2048]{1,0:T(8,128)(2,1)}, bf16[128,2048]{1,0:T(8,128)(2,1)}, bf16[2,128,2048]{2,1,0:T(8,128)(2,1)S(1)}) custom-call(bf16[128,2048]{1,0:T(8,128)(2,1)S(1)} %get-tuple-element.34.query.refs_0, ...), custom_call_target="tpu_custom_call", output_to_operand_aliasing={{0}: (10, {}), {1}: (11, {}), {2}: (12, {}), {3}: (13, {}),... | custom-call | tf_op jit(solution)/shard_map/across_late/pallas_call | solution.py:453
  30.2 0.0 collective-permute-done.11.refs_3_
  30.2 0.3 collective-permute-done.9.refs_1_
  30.5 0.6 %collective-permute-done.10.refs_2_ = bf16[1,128,128]{2,1,0:T(8,128)(2,1)S(1)} collective-permute-done((bf16[1,128,128]{2,1,0:T(8,128)(2,1)S(1)}, bf16[1,128,128]{2,1,0:T(8,128)(2,1)S(1)}, u32[]{:S(2)}, u32[]{:S(2)}) %collective-permute-start.10) | collective-permute-done | bytes 32800 | tf_op jit(solution)/shard_map/ppermute | solution.py:583
  31.1 0.7 %total.1 = f32[128,128]{1,0:T(8,128)} custom-call(bf16[1,128,128]{2,1,0:T(8,128)(2,1)S(1)} %get-tuple-element.53.refs_9_.refs_0_, bf16[1,128,128]{2,1,0:T(8,128)(2,1)S(1)} %collective-permute-done.9.refs_1_, bf16[1,128,128]{2,1,0:T(8,128)(2,1)S(1)} %collective-permute-done.10.refs_2_, bf16[1,128,128]{2,1,0:T(8,128)(2,1)S(1)} %collective-permute-done.11.refs_3_, ...), custom_call_target="tpu_custom_call" | custom-call | tf_op jit(solution)/shard_map/total/pallas_call | solution.py:453
  (1 shorter events, 0.0 us)
Async XLA Ops:
  0.6 2.2 %copy-start = (bf16[1,128,2048]{2,1,0:T(8,128)(2,1)S(1)}, bf16[1,128,2048]{2,1,0:T(8,128)(2,1)}, u32[]{:S(2)}) copy-start(bf16[1,128,2048]{2,1,0:T(8,128)(2,1)} %param.7) | copy-start | bytes 1572868
  0.6 2.2 %copy-start.1 = (bf16[1,128,2048]{2,1,0:T(8,128)(2,1)S(1)}, bf16[1,128,2048]{2,1,0:T(8,128)(2,1)}, u32[]{:S(2)}) copy-start(bf16[1,128,2048]{2,1,0:T(8,128)(2,1)} %param.10) | copy-start | bytes 1572868
  0.7 2.2 %copy-start.2 = (bf16[1,128,2048]{2,1,0:T(8,128)(2,1)S(1)}, bf16[1,128,2048]{2,1,0:T(8,128)(2,1)}, u32[]{:S(2)}) copy-start(bf16[1,128,2048]{2,1,0:T(8,128)(2,1)} %param.8) | copy-start | bytes 1572868
  0.7 2.2 %copy-start.3 = (bf16[1,128,2048]{2,1,0:T(8,128)(2,1)S(1)}, bf16[1,128,2048]{2,1,0:T(8,128)(2,1)}, u32[]{:S(2)}) copy-start(bf16[1,128,2048]{2,1,0:T(8,128)(2,1)} %param.9) | copy-start | bytes 1572868
  2.0 7.6 %copy-start.5 = (bf16[256,256]{1,0:T(8,128)(2,1)S(1)}, bf16[256,256]{1,0:T(8,128)(2,1)}, u32[]{:S(2)}) copy-start(bf16[256,256]{1,0:T(8,128)(2,1)} %constant.4.clone.one.refs_4_) | copy-start | bytes 393220
  2.0 8.6 %collective-permute-start.4 = (bf16[128,1024]{1,0:T(8,128)(2,1)S(1)}, bf16[128,1024]{1,0:T(8,128)(2,1)S(1)}, u32[]{:S(2)}, u32[]{:S(2)}) collective-permute-start(bf16[128,1024]{1,0:T(8,128)(2,1)S(1)} %first.1.refs_4_), channel_id=1, source_target_pairs={{1,2},{3,4},{5,6},{7,8},{9,10},{11,12},{13,14},{2,1},{4,3},{6,5},{... | collective-permute-start | bytes 786440 | tf_op jit(solution)/shard_map/ppermute | solution.py:522
  3.3 5.4 %collective-permute-start = (bf16[128,768]{1,0:T(8,128)(2,1)S(1)}, bf16[128,768]{1,0:T(8,128)(2,1)S(1)}, u32[]{:S(2)}, u32[]{:S(2)}) collective-permute-start(bf16[128,768]{1,0:T(8,128)(2,1)S(1)} %get-tuple-element.38.refs_0_), channel_id=1, source_target_pairs={{0,1},{1,0},{2,3},{3,2},{4,5},{5,4},{6,7},{7,6},{8,9},{9,8},{10,11... | collective-permute-start | bytes 589832 | tf_op jit(solution)/shard_map/ppermute | solution.py:529
  7.6 1.9 %collective-permute-start.1 = (bf16[128,768]{1,0:T(8,128)(2,1)S(1)}, bf16[128,768]{1,0:T(8,128)(2,1)S(1)}, u32[]{:S(2)}, u32[]{:S(2)}) collective-permute-start(bf16[128,768]{1,0:T(8,128)(2,1)S(1)} %get-tuple-element.39.refs_1_), channel_id=1, source_target_pairs={{0,1},{1,0},{2,3},{3,2},{4,5},{5,4},{6,7},{7,6},{8,9},{9,8},{10,11... | collective-permute-start | bytes 589832 | tf_op jit(solution)/shard_map/ppermute | solution.py:529
  7.7 1.8 %collective-permute-start.2 = (bf16[128,768]{1,0:T(8,128)(2,1)S(1)}, bf16[128,768]{1,0:T(8,128)(2,1)S(1)}, u32[]{:S(2)}, u32[]{:S(2)}) collective-permute-start(bf16[128,768]{1,0:T(8,128)(2,1)S(1)} %get-tuple-element.40.refs_2_), channel_id=1, source_target_pairs={{0,1},{1,0},{2,3},{3,2},{4,5},{5,4},{6,7},{7,6},{8,9},{9,8},{10,11... | collective-permute-start | bytes 589832 | tf_op jit(solution)/shard_map/ppermute | solution.py:529
  8.1 1.5 %collective-permute-start.3 = (bf16[128,768]{1,0:T(8,128)(2,1)S(1)}, bf16[128,768]{1,0:T(8,128)(2,1)S(1)}, u32[]{:S(2)}, u32[]{:S(2)}) collective-permute-start(bf16[128,768]{1,0:T(8,128)(2,1)S(1)} %get-tuple-element.41.refs_3_), channel_id=1, source_target_pairs={{0,1},{1,0},{2,3},{3,2},{4,5},{5,4},{6,7},{7,6},{8,9},{9,8},{10,11... | collective-permute-start | bytes 589832 | tf_op jit(solution)/shard_map/ppermute | solution.py:529
  8.7 1.9 %copy-start.4 = (bf16[2,128,768]{2,1,0:T(8,128)(2,1)S(1)}, bf16[2,128,768]{2,1,0:T(8,128)(2,1)}, u32[]{:S(2)}) copy-start(bf16[2,128,768]{2,1,0:T(8,128)(2,1)} %constant.5.clone.lags.refs_5_) | copy-start | bytes 1179652
  8.7 19.1 %collective-permute-start.5 = (bf16[128,1024]{1,0:T(8,128)(2,1)S(1)}, bf16[128,1024]{1,0:T(8,128)(2,1)S(1)}, u32[]{:S(2)}, u32[]{:S(2)}) collective-permute-start(bf16[128,1024]{1,0:T(8,128)(2,1)S(1)} %get-tuple-element.42.base), channel_id=1, source_target_pairs={{1,2},{3,4},{5,6},{7,8},{9,10},{11,12},{13,14},{2,1},{4,3},{6,5},{... | collective-permute-start | bytes 786440 | tf_op jit(solution)/shard_map/ppermute | solution.py:528
  10.6 7.8 %copy-start.6 = (bf16[128,2048]{1,0:T(8,128)(2,1)S(1)}, bf16[128,2048]{1,0:T(8,128)(2,1)}, u32[]{:S(2)}) copy-start(bf16[128,2048]{1,0:T(8,128)(2,1)} %taps_in.1) | copy-start | bytes 1572868
  11.6 11.9 %collective-permute-start.6 = (bf16[2,128,128]{2,1,0:T(8,128)(2,1)S(1)}, bf16[2,128,128]{2,1,0:T(8,128)(2,1)S(1)}, u32[]{:S(2)}, u32[]{:S(2)}) collective-permute-start(bf16[2,128,128]{2,1,0:T(8,128)(2,1)S(1)} %get-tuple-element.48), channel_id=1, source_target_pairs={{0,8},{1,9},{2,10},{3,11},{4,12},{5,13},{6,14},{7,15},{8,0},{9,1},... | collective-permute-start | bytes 196616 | tf_op jit(solution)/shard_map/ppermute | solution.py:571
  16.8 6.7 %collective-permute-start.7 = (bf16[2,128,128]{2,1,0:T(8,128)(2,1)S(1)}, bf16[2,128,128]{2,1,0:T(8,128)(2,1)S(1)}, u32[]{:S(2)}, u32[]{:S(2)}) collective-permute-start(bf16[2,128,128]{2,1,0:T(8,128)(2,1)S(1)} %get-tuple-element.49), channel_id=1, source_target_pairs={{0,12},{1,13},{2,14},{3,15},{4,8},{5,9},{6,10},{7,11},{8,4},{9,5},... | collective-permute-start | bytes 196616 | tf_op jit(solution)/shard_map/ppermute | solution.py:571
  18.2 6.0 %collective-permute-start.8 = (bf16[2,128,128]{2,1,0:T(8,128)(2,1)S(1)}, bf16[2,128,128]{2,1,0:T(8,128)(2,1)S(1)}, u32[]{:S(2)}, u32[]{:S(2)}) collective-permute-start(bf16[2,128,128]{2,1,0:T(8,128)(2,1)S(1)} %get-tuple-element.50), channel_id=1, source_target_pairs={{0,4},{1,5},{2,6},{3,7},{4,0},{5,1},{6,2},{7,3},{8,12},{9,13},{10,... | collective-permute-start | bytes 196616 | tf_op jit(solution)/shard_map/ppermute | solution.py:571
  24.2 6.0 %collective-permute-start.11 = (bf16[1,128,128]{2,1,0:T(8,128)(2,1)S(1)}, bf16[1,128,128]{2,1,0:T(8,128)(2,1)S(1)}, u32[]{:S(2)}, u32[]{:S(2)}) collective-permute-start(bf16[1,128,128]{2,1,0:T(8,128)(2,1)S(1)} %get-tuple-element.62), channel_id=1, source_target_pairs={{0,18},{1,19},{2,16},{3,17},{4,22},{5,23},{6,20},{7,21},{8,26},{9,... | collective-permute-start | bytes 98312 | tf_op jit(solution)/shard_map/ppermute | solution.py:583
  26.6 3.9 %collective-permute-start.9 = (bf16[1,128,128]{2,1,0:T(8,128)(2,1)S(1)}, bf16[1,128,128]{2,1,0:T(8,128)(2,1)S(1)}, u32[]{:S(2)}, u32[]{:S(2)}) collective-permute-start(bf16[1,128,128]{2,1,0:T(8,128)(2,1)S(1)} %get-tuple-element.62), channel_id=1, source_target_pairs={{0,2},{1,3},{2,0},{3,1},{4,6},{5,7},{6,4},{7,5},{8,10},{9,11},{10,... | collective-permute-start | bytes 98312 | tf_op jit(solution)/shard_map/ppermute | solution.py:583
  27.2 3.9 %collective-permute-start.10 = (bf16[1,128,128]{2,1,0:T(8,128)(2,1)S(1)}, bf16[1,128,128]{2,1,0:T(8,128)(2,1)S(1)}, u32[]{:S(2)}, u32[]{:S(2)}) collective-permute-start(bf16[1,128,128]{2,1,0:T(8,128)(2,1)S(1)} %get-tuple-element.53.refs_9_.refs_0_), channel_id=1, source_target_pairs={{0,16},{1,17},{2,18},{3,19},{4,20},{5,21},{6,22},{7,23},{8,24},{9,... | collective-permute-start | bytes 98312 | tf_op jit(solution)/shard_map/ppermute | solution.py:583

commit v4 on v3

--- a/solution.py
+++ b/solution.py
@@ -273,7 +273,8 @@
         for part in arrived:
             value = value + part[place].astype(f32)
         totals[place] = value
-    divide(totals, sends, level)
+    divide(totals, sends[:-1], level)
+    sends[-1][...] = sends[0][...]
 
 
 def total_kernel(scale, *refs):
@@ -575,17 +576,20 @@
         keep, *sends = call(
             functools.partial(join_kernel, left, len(arrived)), "join",
             (keep, *arrived, results[0]),
-            split(left, left is order[-1]),
+            split(left, True) + [shape((left[1], taps, share), bf16)],
             far_ins=(len(arrived) + 1,),
             scratch=[pltpu.VMEM((below, taps, share), f32)],
         )
-    parts = [
-        lax.ppermute(send, ("dp", "ctx"), partner(order[-1], number, over))
-        if number or over
-        else send
-        for over in (0, ctx)
-        for number, send in enumerate([keep] + sends)
+    *sends, twin = sends
+    far_parts = [
+        lax.ppermute(send, ("dp", "ctx"), partner(order[-1], number, ctx))
+        for number, send in enumerate([twin] + sends)
     ]
+    parts = [keep] + [
+        lax.ppermute(send, ("dp", "ctx"), partner(order[-1], number + 1))
+        for number, send in enumerate(sends)
+    ]
+    parts += far_parts
     *results, _ = call(
         functools.partial(across_late_kernel, share), "across_late",
         (*held, late, keep, *results, outer),

time: 32 us -> 31.9 us (level)
  no operation moved by 1% of the time
where the time goes in v4:
time: 31.9 us; the launch traced here: 31.7 us
  starting transfers between devices  16.9 us (53%)
  Pallas kernels  10.8 us (34%)
  waiting for transfers between devices  3.11 us (10%)
  between operations  0.83 us (3%)
    pallas_call x9, Pallas kernels, call(): pl.pallas_call(kernel, in_specs=[pl.BlockSpec(memory_space=space(at)) for...  10.8 us
    ppermute x3, starting transfers between devices, paired(): lax.ppermute(sends[number - 1], ('dp', 'ctx'), partner(level, number))  6.78 us
    ppermute x4, starting transfers between devices, paired(): came = [lax.ppermute(send, 'ctx', inside) for send in sends]  4.96 us
    ppermute x2, starting transfers between devices, paired(): lax.ppermute(send, ('dp', 'ctx'), partner(order[-1], number, ctx))  2.94 us
    ppermute x3, waiting for transfers between devices, paired(): lax.ppermute(sends[number - 1], ('dp', 'ctx'), partner(level, number))  1.66 us
    ppermute x1, starting transfers between devices, paired(): halo = lax.ppermute(urgent, 'ctx', across)  0.81 us
    ppermute x1, starting transfers between devices, paired(): late = lax.ppermute(base, 'ctx', across)  0.8 us
  transfers between devices with their start and end apart: 12, of which 6 were waited for; matrix products, arithmetic and copies ran while one was open for 0% of the time, Pallas kernels for 28%

profile of v4, /device:TPU:0, one launch (start us, length us, event | category | flops | bytes accessed | tf_op | source)
XLA Modules:
  0.0 31.7 jit_solution(17005605808425076927)
XLA Ops:
  0.6 0.0 copy-start
  0.6 0.0 copy-start.1
  0.7 0.0 copy-start.2
  0.7 0.0 copy-start.3
  0.7 1.3 %first.1.refs_4_ = bf16[128,1024]{1,0:T(8,128)(2,1)S(1)} custom-call(bf16[128,2048]{1,0:T(8,128)(2,1)} %bitcast.8, bf16[128,2048]{1,0:T(8,128)(2,1)} %bitcast.10, bf16[128,2048]{1,0:T(8,128)(2,1)} %bitcast.12, bf16[128,2048]{1,0:T(8,128)(2,1)} %bitcast.14), custom_call_target="tpu_custom_call" | custom-call | tf_op jit(solution)/shard_map/first/pallas_call | solution.py:454
  2.0 0.0 copy-start.5
  2.0 0.8 %collective-permute-start.4 = (bf16[128,1024]{1,0:T(8,128)(2,1)S(1)}, bf16[128,1024]{1,0:T(8,128)(2,1)S(1)}, u32[]{:S(2)}, u32[]{:S(2)}) collective-permute-start(bf16[128,1024]{1,0:T(8,128)(2,1)S(1)} %first.1.refs_4_), channel_id=1, source_target_pairs={{1,2},{3,4},{5,6},{7,8},{9,10},{11,12},{13,14},{2,1},{4,3},{6,5},{... | collective-permute-start | bytes 786440 | tf_op jit(solution)/shard_map/ppermute | solution.py:523
  2.8 0.0 copy-done
  2.8 0.0 copy-done.1
  2.8 0.0 copy-done.2
  2.9 0.0 copy-done.3
  2.9 0.4 %prepare.1 = (bf16[128,2048]{1,0:T(8,128)(2,1)S(1)}, bf16[128,2048]{1,0:T(8,128)(2,1)S(1)}, bf16[128,2048]{1,0:T(8,128)(2,1)S(1)}, bf16[128,2048]{1,0:T(8,128)(2...) custom-call(bf16[128,2048]{1,0:T(8,128)(2,1)S(1)} %bitcast.9, ...), custom_call_target="tpu_custom_call" | custom-call | tf_op jit(solution)/shard_map/prepare/pallas_call | solution.py:454
  3.3 4.4 %collective-permute-start = (bf16[128,768]{1,0:T(8,128)(2,1)S(1)}, bf16[128,768]{1,0:T(8,128)(2,1)S(1)}, u32[]{:S(2)}, u32[]{:S(2)}) collective-permute-start(bf16[128,768]{1,0:T(8,128)(2,1)S(1)} %get-tuple-element.39.refs_0_), channel_id=1, source_target_pairs={{0,1},{1,0},{2,3},{3,2},{4,5},{5,4},{6,7},{7,6},{8,9},{9,8},{10,11... | collective-permute-start | bytes 589832 | tf_op jit(solution)/shard_map/ppermute | solution.py:530
  7.6 0.1 collective-permute-start.1
  7.7 0.4 %collective-permute-start.2 = (bf16[128,768]{1,0:T(8,128)(2,1)S(1)}, bf16[128,768]{1,0:T(8,128)(2,1)S(1)}, u32[]{:S(2)}, u32[]{:S(2)}) collective-permute-start(bf16[128,768]{1,0:T(8,128)(2,1)S(1)} %get-tuple-element.41.refs_2_), channel_id=1, source_target_pairs={{0,1},{1,0},{2,3},{3,2},{4,5},{5,4},{6,7},{7,6},{8,9},{9,8},{10,11... | collective-permute-start | bytes 589832 | tf_op jit(solution)/shard_map/ppermute | solution.py:530
  8.1 0.1 collective-permute-start.3
  8.2 0.5 %collective-permute-done.refs_4_.refs_0_ = bf16[128,768]{1,0:T(8,128)(2,1)S(1)} collective-permute-done((bf16[128,768]{1,0:T(8,128)(2,1)S(1)}, bf16[128,768]{1,0:T(8,128)(2,1)S(1)}, u32[]{:S(2)}, u32[]{:S(2)}) %collective-permute-start) | collective-permute-done | bytes 196640 | tf_op jit(solution)/shard_map/ppermute | solution.py:530
  8.7 0.0 copy-start.4
  8.7 0.8 %collective-permute-start.5 = (bf16[128,1024]{1,0:T(8,128)(2,1)S(1)}, bf16[128,1024]{1,0:T(8,128)(2,1)S(1)}, u32[]{:S(2)}, u32[]{:S(2)}) collective-permute-start(bf16[128,1024]{1,0:T(8,128)(2,1)S(1)} %get-tuple-element.43.base), channel_id=1, source_target_pairs={{1,2},{3,4},{5,6},{7,8},{9,10},{11,12},{13,14},{2,1},{4,3},{6,5},{... | collective-permute-start | bytes 786440 | tf_op jit(solution)/shard_map/ppermute | solution.py:529
  9.5 0.0 collective-permute-done.1.refs_5_.refs_1_
  9.5 0.0 collective-permute-done.2.refs_6_.refs_2_
  9.5 0.1 collective-permute-done.3.refs_7_.refs_3_
  9.6 0.0 copy-done.5
  9.6 1.0 %inside.1 = (f32[256,1024]{1,0:T(8,128)S(1)}, f32[256,1024]{1,0:T(8,128)S(1)}) custom-call(bf16[256,256]{1,0:T(8,128)(2,1)S(1)} %copy-done.5, bf16[128,1024]{1,0:T(8,128)(2,1)S(1)} %get-tuple-element.43.base, bf16[128,768]{1,0:T(8,128)(2,1)S(1)} %get-tuple-element.39.refs_0_, bf16[128,768]{1,0:T(8,128)(2,1)S(1)} %get-tuple-element.40.refs_1_, ...), custom_call_target="tpu_custom_call" | custom-call | tf_op jit(solution)/shard_map/inside/pallas_call | solution.py:454
  10.6 0.0 collective-permute-done.4.halo.refs_8_
  10.6 0.0 copy-done.4
  10.6 0.0 copy-start.6
  10.6 1.0 %lags.3 = (f32[2,128,128]{2,1,0:T(8,128)S(1)}, bf16[2,128,128]{2,1,0:T(8,128)(2,1)S(1)}, bf16[2,128,128]{2,1,0:T(8,128)(2,1)S(1)}, bf16[2,128,128]{2,1,0:T(8,128)(2,1)S(1)}) custom-call(bf16[256,256]{1,0:T(8,128)(2,1)S(1)} %copy-done.5, bf16[2,128,768]{2,1,0:T(8,128)(2,1)S(1)} %copy-done.4, bf16[128,1024]{1,0:T(8,128)(2,1)S(1)} %collective-permute-done.4.halo.refs_8_, ...), custom_call_target="tpu_custom_call" | custom-call | tf_op jit(solution)/shard_map/lags/pallas_call | solution.py:454
  11.6 5.2 %collective-permute-start.6 = (bf16[2,128,128]{2,1,0:T(8,128)(2,1)S(1)}, bf16[2,128,128]{2,1,0:T(8,128)(2,1)S(1)}, u32[]{:S(2)}, u32[]{:S(2)}) collective-permute-start(bf16[2,128,128]{2,1,0:T(8,128)(2,1)S(1)} %get-tuple-element.49), channel_id=1, source_target_pairs={{0,8},{1,9},{2,10},{3,11},{4,12},{5,13},{6,14},{7,15},{8,0},{9,1},... | collective-permute-start | bytes 196616 | tf_op jit(solution)/shard_map/ppermute | solution.py:572
  16.8 1.3 %collective-permute-start.7 = (bf16[2,128,128]{2,1,0:T(8,128)(2,1)S(1)}, bf16[2,128,128]{2,1,0:T(8,128)(2,1)S(1)}, u32[]{:S(2)}, u32[]{:S(2)}) collective-permute-start(bf16[2,128,128]{2,1,0:T(8,128)(2,1)S(1)} %get-tuple-element.50), channel_id=1, source_target_pairs={{0,12},{1,13},{2,14},{3,15},{4,8},{5,9},{6,10},{7,11},{8,4},{9,5},... | collective-permute-start | bytes 196616 | tf_op jit(solution)/shard_map/ppermute | solution.py:572
  18.2 0.2 collective-permute-start.8
  18.4 0.0 copy-done.6
  18.4 2.4 %inside_way.1 = (bf16[2,128,2048]{2,1,0:T(8,128)(2,1)S(1)}, bf16[256,512]{1,0:T(8,128)(2,1)S(1)}, bf16[128,2048]{1,0:T(8,128)(2,1)S(1)}) custom-call(bf16[128,2048]{1,0:T(8,128)(2,1)S(1)} %get-tuple-element.35.query.refs_0_, bf16[128,2048]{1,0:T(8,128)(2,1)S(1)} %get-tuple-element.36.key.refs_1_, bf16[128,2048]{1,0:T(8,128)(2,1)S(1)} %get-tuple-element.37.value.refs_2_, ...), custom_call_target="tpu_custom_call" | custom-call | flops 3000000000 | tf_op jit(solution)/shard_map/inside_way/pallas_call | solution.py:454
  20.8 1.7 %across_first.1 = (bf16[128,2048]{1,0:T(8,128)(2,1)}, bf16[128,2048]{1,0:T(8,128)(2,1)}, bf16[128,2048]{1,0:T(8,128)(2,1)}, bf16[128,2048]{1,0:T(8,128)(2,1)}, bf16[2,128,2048]{2,1,0:T(8,128)(2,1)S(1)}) custom-call(bf16[128,2048]{1,0:T(8,128)(2,1)S(1)} %get-tuple-element.35.query.refs_0_, bf16[128,2048]{1,0:T(8,128)(2,1)S(1)} %get-tuple-element.36.key.refs_1_, ...), custom_call_target="tpu_custom_call" | custom-call | flops 3000000000 | tf_op jit(solution)/shard_map/across_first/pallas_call | solution.py:454
  22.5 1.0 %collective-permute-done.6.refs_0_ = bf16[2,128,128]{2,1,0:T(8,128)(2,1)S(1)} collective-permute-done((bf16[2,128,128]{2,1,0:T(8,128)(2,1)S(1)}, bf16[2,128,128]{2,1,0:T(8,128)(2,1)S(1)}, u32[]{:S(2)}, u32[]{:S(2)}) %collective-permute-start.6) | collective-permute-done | bytes 65568 | tf_op jit(solution)/shard_map/ppermute | solution.py:572
  23.5 0.0 collective-permute-done.7.refs_1_
  23.5 0.6 %collective-permute-done.8.refs_2_ = bf16[2,128,128]{2,1,0:T(8,128)(2,1)S(1)} collective-permute-done((bf16[2,128,128]{2,1,0:T(8,128)(2,1)S(1)}, bf16[2,128,128]{2,1,0:T(8,128)(2,1)S(1)}, u32[]{:S(2)}, u32[]{:S(2)}) %collective-permute-start.8) | collective-permute-done | bytes 65568 | tf_op jit(solution)/shard_map/ppermute | solution.py:572
  24.2 1.6 %collective-permute-start.10 = (bf16[1,128,128]{2,1,0:T(8,128)(2,1)S(1)}, bf16[1,128,128]{2,1,0:T(8,128)(2,1)S(1)}, u32[]{:S(2)}, u32[]{:S(2)}) collective-permute-start(bf16[1,128,128]{2,1,0:T(8,128)(2,1)S(1)} %get-tuple-element.64), channel_id=1, source_target_pairs={{0,16},{1,17},{2,18},{3,19},{4,20},{5,21},{6,22},{7,23},{8,24},{9,... | collective-permute-start | bytes 98312 | tf_op jit(solution)/shard_map/ppermute | solution.py:585
  25.8 1.4 %collective-permute-start.11 = (bf16[1,128,128]{2,1,0:T(8,128)(2,1)S(1)}, bf16[1,128,128]{2,1,0:T(8,128)(2,1)S(1)}, u32[]{:S(2)}, u32[]{:S(2)}) collective-permute-start(bf16[1,128,128]{2,1,0:T(8,128)(2,1)S(1)} %get-tuple-element.63), channel_id=1, source_target_pairs={{0,18},{1,19},{2,16},{3,17},{4,22},{5,23},{6,20},{7,21},{8,26},{9,... | collective-permute-start | bytes 98312 | tf_op jit(solution)/shard_map/ppermute | solution.py:585
  27.1 0.6 %collective-permute-start.9 = (bf16[1,128,128]{2,1,0:T(8,128)(2,1)S(1)}, bf16[1,128,128]{2,1,0:T(8,128)(2,1)S(1)}, u32[]{:S(2)}, u32[]{:S(2)}) collective-permute-start(bf16[1,128,128]{2,1,0:T(8,128)(2,1)S(1)} %get-tuple-element.63), channel_id=1, source_target_pairs={{0,2},{1,3},{2,0},{3,1},{4,6},{5,7},{6,4},{7,5},{8,10},{9,11},{10,... | collective-permute-start | bytes 98312 | tf_op jit(solution)/shard_map/ppermute | solution.py:589
  27.8 0.0 collective-permute-done.5.refs_8_
  27.8 2.4 %across_late.1 = (bf16[128,2048]{1,0:T(8,128)(2,1)}, bf16[128,2048]{1,0:T(8,128)(2,1)}, bf16[128,2048]{1,0:T(8,128)(2,1)}, bf16[128,2048]{1,0:T(8,128)(2,1)}, bf16[2,128,2048]{2,1,0:T(8,128)(2,1)S(1)}) custom-call(bf16[128,2048]{1,0:T(8,128)(2,1)S(1)} %get-tuple-element.35.query.refs_0, ...), custom_call_target="tpu_custom_call", output_to_operand_aliasing={{0}: (10, {}), {1}: (11, {}), {2}: (12, {}), {3}: (13, {}),... | custom-call | tf_op jit(solution)/shard_map/across_late/pallas_call | solution.py:454
  30.2 0.0 collective-permute-done.10.refs_2_
  30.2 0.4 %collective-permute-done.11.refs_3_ = bf16[1,128,128]{2,1,0:T(8,128)(2,1)S(1)} collective-permute-done((bf16[1,128,128]{2,1,0:T(8,128)(2,1)S(1)}, bf16[1,128,128]{2,1,0:T(8,128)(2,1)S(1)}, u32[]{:S(2)}, u32[]{:S(2)}) %collective-permute-start.11) | collective-permute-done | bytes 32800 | tf_op jit(solution)/shard_map/ppermute | solution.py:585
  30.6 0.5 %collective-permute-done.9.refs_1_ = bf16[1,128,128]{2,1,0:T(8,128)(2,1)S(1)} collective-permute-done((bf16[1,128,128]{2,1,0:T(8,128)(2,1)S(1)}, bf16[1,128,128]{2,1,0:T(8,128)(2,1)S(1)}, u32[]{:S(2)}, u32[]{:S(2)}) %collective-permute-start.9) | collective-permute-done | bytes 32800 | tf_op jit(solution)/shard_map/ppermute | solution.py:589
  31.1 0.7 %total.1 = f32[128,128]{1,0:T(8,128)} custom-call(bf16[1,128,128]{2,1,0:T(8,128)(2,1)S(1)} %get-tuple-element.54.refs_9_.refs_0_, bf16[1,128,128]{2,1,0:T(8,128)(2,1)S(1)} %collective-permute-done.9.refs_1_, bf16[1,128,128]{2,1,0:T(8,128)(2,1)S(1)} %collective-permute-done.10.refs_2_, bf16[1,128,128]{2,1,0:T(8,128)(2,1)S(1)} %collective-permute-done.11.refs_3_, ...), custom_call_target="tpu_custom_call" | custom-call | tf_op jit(solution)/shard_map/total/pallas_call | solution.py:454
  (1 shorter events, 0.0 us)
Async XLA Ops:
  0.6 2.2 %copy-start = (bf16[1,128,2048]{2,1,0:T(8,128)(2,1)S(1)}, bf16[1,128,2048]{2,1,0:T(8,128)(2,1)}, u32[]{:S(2)}) copy-start(bf16[1,128,2048]{2,1,0:T(8,128)(2,1)} %param.7) | copy-start | bytes 1572868
  0.6 2.2 %copy-start.1 = (bf16[1,128,2048]{2,1,0:T(8,128)(2,1)S(1)}, bf16[1,128,2048]{2,1,0:T(8,128)(2,1)}, u32[]{:S(2)}) copy-start(bf16[1,128,2048]{2,1,0:T(8,128)(2,1)} %param.10) | copy-start | bytes 1572868
  0.7 2.2 %copy-start.2 = (bf16[1,128,2048]{2,1,0:T(8,128)(2,1)S(1)}, bf16[1,128,2048]{2,1,0:T(8,128)(2,1)}, u32[]{:S(2)}) copy-start(bf16[1,128,2048]{2,1,0:T(8,128)(2,1)} %param.8) | copy-start | bytes 1572868
  0.7 2.2 %copy-start.3 = (bf16[1,128,2048]{2,1,0:T(8,128)(2,1)S(1)}, bf16[1,128,2048]{2,1,0:T(8,128)(2,1)}, u32[]{:S(2)}) copy-start(bf16[1,128,2048]{2,1,0:T(8,128)(2,1)} %param.9) | copy-start | bytes 1572868
  2.0 7.6 %copy-start.5 = (bf16[256,256]{1,0:T(8,128)(2,1)S(1)}, bf16[256,256]{1,0:T(8,128)(2,1)}, u32[]{:S(2)}) copy-start(bf16[256,256]{1,0:T(8,128)(2,1)} %constant.4.clone.one.refs_4_) | copy-start | bytes 393220
  2.0 8.6 %collective-permute-start.4 = (bf16[128,1024]{1,0:T(8,128)(2,1)S(1)}, bf16[128,1024]{1,0:T(8,128)(2,1)S(1)}, u32[]{:S(2)}, u32[]{:S(2)}) collective-permute-start(bf16[128,1024]{1,0:T(8,128)(2,1)S(1)} %first.1.refs_4_), channel_id=1, source_target_pairs={{1,2},{3,4},{5,6},{7,8},{9,10},{11,12},{13,14},{2,1},{4,3},{6,5},{... | collective-permute-start | bytes 786440 | tf_op jit(solution)/shard_map/ppermute | solution.py:523
  3.3 5.4 %collective-permute-start = (bf16[128,768]{1,0:T(8,128)(2,1)S(1)}, bf16[128,768]{1,0:T(8,128)(2,1)S(1)}, u32[]{:S(2)}, u32[]{:S(2)}) collective-permute-start(bf16[128,768]{1,0:T(8,128)(2,1)S(1)} %get-tuple-element.39.refs_0_), channel_id=1, source_target_pairs={{0,1},{1,0},{2,3},{3,2},{4,5},{5,4},{6,7},{7,6},{8,9},{9,8},{10,11... | collective-permute-start | bytes 589832 | tf_op jit(solution)/shard_map/ppermute | solution.py:530
  7.6 1.9 %collective-permute-start.1 = (bf16[128,768]{1,0:T(8,128)(2,1)S(1)}, bf16[128,768]{1,0:T(8,128)(2,1)S(1)}, u32[]{:S(2)}, u32[]{:S(2)}) collective-permute-start(bf16[128,768]{1,0:T(8,128)(2,1)S(1)} %get-tuple-element.40.refs_1_), channel_id=1, source_target_pairs={{0,1},{1,0},{2,3},{3,2},{4,5},{5,4},{6,7},{7,6},{8,9},{9,8},{10,11... | collective-permute-start | bytes 589832 | tf_op jit(solution)/shard_map/ppermute | solution.py:530
  7.7 1.8 %collective-permute-start.2 = (bf16[128,768]{1,0:T(8,128)(2,1)S(1)}, bf16[128,768]{1,0:T(8,128)(2,1)S(1)}, u32[]{:S(2)}, u32[]{:S(2)}) collective-permute-start(bf16[128,768]{1,0:T(8,128)(2,1)S(1)} %get-tuple-element.41.refs_2_), channel_id=1, source_target_pairs={{0,1},{1,0},{2,3},{3,2},{4,5},{5,4},{6,7},{7,6},{8,9},{9,8},{10,11... | collective-permute-start | bytes 589832 | tf_op jit(solution)/shard_map/ppermute | solution.py:530
  8.1 1.5 %collective-permute-start.3 = (bf16[128,768]{1,0:T(8,128)(2,1)S(1)}, bf16[128,768]{1,0:T(8,128)(2,1)S(1)}, u32[]{:S(2)}, u32[]{:S(2)}) collective-permute-start(bf16[128,768]{1,0:T(8,128)(2,1)S(1)} %get-tuple-element.42.refs_3_), channel_id=1, source_target_pairs={{0,1},{1,0},{2,3},{3,2},{4,5},{5,4},{6,7},{7,6},{8,9},{9,8},{10,11... | collective-permute-start | bytes 589832 | tf_op jit(solution)/shard_map/ppermute | solution.py:530
  8.7 1.9 %copy-start.4 = (bf16[2,128,768]{2,1,0:T(8,128)(2,1)S(1)}, bf16[2,128,768]{2,1,0:T(8,128)(2,1)}, u32[]{:S(2)}) copy-start(bf16[2,128,768]{2,1,0:T(8,128)(2,1)} %constant.5.clone.lags.refs_5_) | copy-start | bytes 1179652
  8.7 19.1 %collective-permute-start.5 = (bf16[128,1024]{1,0:T(8,128)(2,1)S(1)}, bf16[128,1024]{1,0:T(8,128)(2,1)S(1)}, u32[]{:S(2)}, u32[]{:S(2)}) collective-permute-start(bf16[128,1024]{1,0:T(8,128)(2,1)S(1)} %get-tuple-element.43.base), channel_id=1, source_target_pairs={{1,2},{3,4},{5,6},{7,8},{9,10},{11,12},{13,14},{2,1},{4,3},{6,5},{... | collective-permute-start | bytes 786440 | tf_op jit(solution)/shard_map/ppermute | solution.py:529
  10.6 7.8 %copy-start.6 = (bf16[128,2048]{1,0:T(8,128)(2,1)S(1)}, bf16[128,2048]{1,0:T(8,128)(2,1)}, u32[]{:S(2)}) copy-start(bf16[128,2048]{1,0:T(8,128)(2,1)} %taps_in.1) | copy-start | bytes 1572868
  11.6 11.9 %collective-permute-start.6 = (bf16[2,128,128]{2,1,0:T(8,128)(2,1)S(1)}, bf16[2,128,128]{2,1,0:T(8,128)(2,1)S(1)}, u32[]{:S(2)}, u32[]{:S(2)}) collective-permute-start(bf16[2,128,128]{2,1,0:T(8,128)(2,1)S(1)} %get-tuple-element.49), channel_id=1, source_target_pairs={{0,8},{1,9},{2,10},{3,11},{4,12},{5,13},{6,14},{7,15},{8,0},{9,1},... | collective-permute-start | bytes 196616 | tf_op jit(solution)/shard_map/ppermute | solution.py:572
  16.8 6.7 %collective-permute-start.7 = (bf16[2,128,128]{2,1,0:T(8,128)(2,1)S(1)}, bf16[2,128,128]{2,1,0:T(8,128)(2,1)S(1)}, u32[]{:S(2)}, u32[]{:S(2)}) collective-permute-start(bf16[2,128,128]{2,1,0:T(8,128)(2,1)S(1)} %get-tuple-element.50), channel_id=1, source_target_pairs={{0,12},{1,13},{2,14},{3,15},{4,8},{5,9},{6,10},{7,11},{8,4},{9,5},... | collective-permute-start | bytes 196616 | tf_op jit(solution)/shard_map/ppermute | solution.py:572
  18.2 6.0 %collective-permute-start.8 = (bf16[2,128,128]{2,1,0:T(8,128)(2,1)S(1)}, bf16[2,128,128]{2,1,0:T(8,128)(2,1)S(1)}, u32[]{:S(2)}, u32[]{:S(2)}) collective-permute-start(bf16[2,128,128]{2,1,0:T(8,128)(2,1)S(1)} %get-tuple-element.51), channel_id=1, source_target_pairs={{0,4},{1,5},{2,6},{3,7},{4,0},{5,1},{6,2},{7,3},{8,12},{9,13},{10,... | collective-permute-start | bytes 196616 | tf_op jit(solution)/shard_map/ppermute | solution.py:572
  24.2 6.0 %collective-permute-start.10 = (bf16[1,128,128]{2,1,0:T(8,128)(2,1)S(1)}, bf16[1,128,128]{2,1,0:T(8,128)(2,1)S(1)}, u32[]{:S(2)}, u32[]{:S(2)}) collective-permute-start(bf16[1,128,128]{2,1,0:T(8,128)(2,1)S(1)} %get-tuple-element.64), channel_id=1, source_target_pairs={{0,16},{1,17},{2,18},{3,19},{4,20},{5,21},{6,22},{7,23},{8,24},{9,... | collective-permute-start | bytes 98312 | tf_op jit(solution)/shard_map/ppermute | solution.py:585
  25.8 4.8 %collective-permute-start.11 = (bf16[1,128,128]{2,1,0:T(8,128)(2,1)S(1)}, bf16[1,128,128]{2,1,0:T(8,128)(2,1)S(1)}, u32[]{:S(2)}, u32[]{:S(2)}) collective-permute-start(bf16[1,128,128]{2,1,0:T(8,128)(2,1)S(1)} %get-tuple-element.63), channel_id=1, source_target_pairs={{0,18},{1,19},{2,16},{3,17},{4,22},{5,23},{6,20},{7,21},{8,26},{9,... | collective-permute-start | bytes 98312 | tf_op jit(solution)/shard_map/ppermute | solution.py:585
  27.1 3.9 %collective-permute-start.9 = (bf16[1,128,128]{2,1,0:T(8,128)(2,1)S(1)}, bf16[1,128,128]{2,1,0:T(8,128)(2,1)S(1)}, u32[]{:S(2)}, u32[]{:S(2)}) collective-permute-start(bf16[1,128,128]{2,1,0:T(8,128)(2,1)S(1)} %get-tuple-element.63), channel_id=1, source_target_pairs={{0,2},{1,3},{2,0},{3,1},{4,6},{5,7},{6,4},{7,5},{8,10},{9,11},{10,... | collective-permute-start | bytes 98312 | tf_op jit(solution)/shard_map/ppermute | solution.py:589
